TPU v7x, 32 devices: a whole 2x2x4 slice. The times are simulated.
32 devices in a mesh: band: 8 (over y, x, core), slab: 4 (over z).
Axes of the slice: x: 2, y: 2, z: 4, core: 2. Of those that a mesh axis runs over, the one named last changes fastest.
Arguments:
- wave_coeffs: float32 [16, 2, 128, 128, 128], P('band', None, 'slab'), may hold values from -12 to 12
- column_mask: int32 [128, 128], replicated, may hold values from 0 to 1, as said below
- occupations: float32 [16], P('band'), may hold values from 0.1 to 2
- core_density: float32 [128, 128, 128], P('band', 'slab'), may hold values from 0.05 to 0.5
Outputs:
- hartree: float32 [128, 128, 128], P('band', 'slab')
- xc_potential: float32 [128, 128, 128], P('band', 'slab')
Inputs may be any that keep to these rules, and one draw needn't show every extreme that they name: `column_mask`: 1 marks a column of frequencies (first two indices) inside the cutoff; only columns whose shifted indices s1, s2 satisfy s1^2 + s2^2 <= 32^2 can be 1.
All inputs are finite; a program needn't handle non-finite values.
Results may differ from a plain program's by a relative error of at most 0.00035.
Values sent between devices are 32-bit elements; how exact they have to be, the bound alone decides.
A program may use at most 64 MiB of HBM per device.

v0:
```python
import math

import jax
import jax.numpy as jnp
from jax import lax
from jax.sharding import PartitionSpec as P

grid_spacing = 0.59
wigner_a = 0.44
wigner_b = 7.8


def dft_tables(extent):
    indices = jnp.arange(extent, dtype=jnp.int32)
    phase = indices[:, None] * indices[None, :] % extent
    angle = phase.astype(jnp.float32) * (2.0 * math.pi / extent)
    return (jnp.cos(angle), jnp.sin(angle))


def kernel_block(extent, starts, amounts):
    pieces = []
    for offset, amount in zip(starts, amounts):
        frequency = offset + jnp.arange(amount, dtype=jnp.int32)
        shifted = (frequency + extent // 2) % extent - extent // 2
        pieces.append(shifted * shifted)
    squared = pieces[0][:, None, None] + pieces[1][None, :, None] + pieces[2][None, None, :]
    length = extent * grid_spacing
    scaled = length * length / math.pi / jnp.maximum(squared, 1).astype(jnp.float32)
    return jnp.where(squared == 0, 0.0, scaled)


def exchange_correlation(density):
    root_density = jnp.cbrt(density)
    radius = (3.0 / (4.0 * math.pi)) ** (1.0 / 3.0) / root_density
    exchange_part = -((3.0 / math.pi) ** (1.0 / 3.0)) * root_density
    shifted = radius + wigner_b
    correlation = -wigner_a / shifted - wigner_a * radius / (3.0 * shifted * shifted)
    return exchange_part + correlation


def project(pattern, values, matrix):
    return jnp.einsum(pattern, values, matrix, precision=lax.Precision.HIGHEST)


def rotate(real_part, imag_part, pattern, cosine_table, sine_table, direction):
    new_real = project(pattern, real_part, cosine_table) - direction * project(
        pattern, imag_part, sine_table
    )
    new_imag = direction * project(pattern, real_part, sine_table) + project(
        pattern, imag_part, cosine_table
    )
    return (new_real, new_imag)


def local(wave_coeffs, column_mask, occupations, core_density):
    local_bands = wave_coeffs.shape[0]
    row_count = wave_coeffs.shape[2]
    extent = wave_coeffs.shape[3]
    bands_all = lax.axis_size("band") * local_bands
    band_rows = extent // lax.axis_size("band")
    slab_index = lax.axis_index("slab")
    band_index = lax.axis_index("band")
    cosine_table, sine_table = dft_tables(extent)
    mask_rows = lax.dynamic_slice_in_dim(column_mask, slab_index * row_count, row_count, 0).astype(
        jnp.float32
    )
    masked = wave_coeffs * mask_rows[None, None, :, :, None]
    real_part, imag_part = rotate(
        masked[:, 0], masked[:, 1], "bxyz,zw->bxyw", cosine_table, sine_table, 1.0
    )
    real_part, imag_part = rotate(
        real_part, imag_part, "bxyz,yw->bxwz", cosine_table, sine_table, 1.0
    )
    stacked = jnp.stack((real_part, imag_part), axis=1)
    factor = 1.0 / (float(extent) ** 3 * bands_all)
    partial_value = jnp.zeros((extent, row_count, extent), jnp.float32)
    for member in range(local_bands):
        arrived = lax.all_to_all(stacked[member], "slab", split_axis=2, concat_axis=1, tiled=True)
        plane_real, plane_imag = rotate(
            arrived[0], arrived[1], "xyz,xw->wyz", cosine_table, sine_table, 1.0
        )
        partial_value = partial_value + occupations[member] * (
            plane_real * plane_real + plane_imag * plane_imag
        )
    partial_value = partial_value * factor
    density = lax.psum(partial_value, "band")
    own_density = lax.dynamic_slice_in_dim(density, band_index * band_rows, band_rows, 0)
    first_real = project("xyz,zw->xyw", density, cosine_table)
    first_imag = -project("xyz,zw->xyw", density, sine_table)
    line_real, line_imag = rotate(
        first_real, first_imag, "xyz,xw->wyz", cosine_table, sine_table, -1.0
    )
    arrived = lax.all_to_all(
        jnp.stack((line_real, line_imag)), "slab", split_axis=1, concat_axis=2, tiled=True
    )
    line_real, line_imag = rotate(
        arrived[0], arrived[1], "xyz,yw->xwz", cosine_table, sine_table, -1.0
    )
    kernel = kernel_block(extent, (slab_index * row_count, 0, 0), (row_count, extent, extent))
    line_real, line_imag = rotate(
        kernel * line_real, kernel * line_imag, "xyz,yw->xwz", cosine_table, sine_table, 1.0
    )
    arrived = lax.all_to_all(
        jnp.stack((line_real, line_imag)), "slab", split_axis=2, concat_axis=1, tiled=True
    )
    cosine_rows = lax.dynamic_slice_in_dim(cosine_table, band_index * band_rows, band_rows, 1)
    sine_rows = lax.dynamic_slice_in_dim(sine_table, band_index * band_rows, band_rows, 1)
    line_real, line_imag = rotate(
        arrived[0], arrived[1], "xyz,xw->wyz", cosine_rows, sine_rows, 1.0
    )
    spatial = project("xyz,zw->xyw", line_real, cosine_table) - project(
        "xyz,zw->xyw", line_imag, sine_table
    )
    hartree = spatial / float(extent) ** 3
    xc_potential = exchange_correlation(own_density + core_density)
    return (hartree, xc_potential)


def solution(mesh):
    return jax.shard_map(
        local,
        mesh=mesh,
        in_specs=(P("band", None, "slab", None, None), P(), P("band"), P("band", "slab", None)),
        out_specs=(P("band", "slab", None), P("band", "slab", None)),
        check_vma=False,
    )
```

profile of v0, /device:TPU:0, one launch (start us, length us, event | category | flops | bytes accessed | tf_op | source)
XLA Modules:
  0.0 600.5 jit_solution(9763391334923213450)
XLA Ops:
  7.2 0.7 dynamic-slice_convert_fusion
  7.9 4.2 copy_multiply_fusion
  12.1 3.7 fusion.3
  15.8 3.7 fusion.4
  19.5 3.7 fusion.7
  23.2 4.3 fusion.71
  27.4 4.0 fusion.68
  31.5 3.7 fusion.8
  35.2 13.7 %subtract_bitcast_fusion = f32[2,1,32,128,128]{4,3,2,0,1:T(8,128)S(1)} fusion(f32[128,2,32,128]{3,0,2,1:T(8,128)S(1)} %fusion.68, f32[2,32,128,128]{3,2,1,0:T(8,128)S(1)} %fusion.8), kind=kOutput, calls=%fused_computation.15 | convolution fusion | flops 1611890688 | bytes 12582912 | tf_op jit(solution)/shard_map/bxyz,yw->bxwz/dot_general | solution.py:42
  48.8 4.0 add_bitcast_fusion
  52.9 2.4 fusion.1
  55.3 4.4 copy.102
  59.7 6.3 %all-to-all-start = ((f32[2,32,128,128]{3,1,0,2:T(8,128)}), f32[2,32,128,128]{3,1,0,2:T(8,128)}, u32[]{:S(2)}, u32[]{:S(2)}) async-start(f32[2,32,128,128]{3,1,0,2:T(8,128)} %copy.102), calls=%async_computation | async-start | bytes 8388608 | tf_op jit(solution)/shard_map/all_to_all | solution.py:78
  66.0 6.6 %copy.104 = f32[2,32,128,128]{3,1,0,2:T(8,128)} copy(f32[2,32,128,128]{3,2,1,0:T(8,128)} %get-tuple-element.11) | data formatting | bytes 8388608 | tf_op jit(solution)/shard_map/squeeze | solution.py:78
  72.6 86.8 %all-to-all-done = f32[2,32,128,128]{3,1,0,2:T(8,128)} async-done(((f32[2,32,128,128]{3,1,0,2:T(8,128)}), f32[2,32,128,128]{3,1,0,2:T(8,128)}, u32[]{:S(2)}, u32[]{:S(2)}) %all-to-all-start) | async-done | bytes 4194336 | tf_op jit(solution)/shard_map/all_to_all | solution.py:78
  159.4 4.8 all-to-all-start.1
  164.7 0.6 fusion.281
  165.3 2.8 copy.169
  168.1 0.8 fusion.279
  169.0 2.1 fusion.61
  171.1 3.5 fusion.92
  174.6 3.5 fusion.90
  178.1 3.5 fusion.63
  181.6 75.3 %all-to-all-done.1 = f32[2,32,128,128]{3,1,0,2:T(8,128)} async-done(((f32[2,32,128,128]{3,1,0,2:T(8,128)}), f32[2,32,128,128]{3,1,0,2:T(8,128)}, u32[]{:S(2)}, u32[]{:S(2)}) %all-to-all-start.1) | async-done | bytes 4194336 | tf_op jit(solution)/shard_map/all_to_all | solution.py:78
  256.9 2.7 copy.168
  259.5 0.6 fusion.280
  260.2 2.1 fusion.57
  262.5 2.2 fusion.88
  264.7 2.2 fusion.59
  266.9 6.0 %add_multiply_fusion = f32[128,32,128]{2,0,1:T(8,128)} fusion(f32[128,32,128]{2,0,1:T(8,128)S(1)} %fusion.57, f32[128,32,128]{2,0,1:T(8,128)S(1)} %fusion.88, f32[128,32,128]{2,0,1:T(8,128)S(1)} %fusion.59, f32[128,32,128]{2,0,1:T(8,128)S(1)} %fusion.61, f32[128,32,128]{2,0,1:T(8,128)S(1)} %copy-done.2, f32[128,32,128]{2,0,1:T(8,128)S(1)} %copy-done.1, ...), kind=kOutput, calls=%fused_computation.33 | convolution fusion | flops 812875776 | bytes 18874376 | tf_op jit(solution)/shard_map/xyz,xw->wyz/dot_general | solution.py:42
  273.0 61.0 %all-reduce.2.cloned.1.call-done = f32[128,32,128]{2,0,1:T(8,128)} async-done(((f32[128,32,128]{2,0,1:T(8,128)}), f32[128,32,128]{2,0,1:T(8,128)}) %all-reduce.2.cloned.1.call-update) | async-done | bytes 2097168 | tf_op jit(solution)/shard_map/psum | solution.py:86
  333.9 3.7 fusion.76
  337.6 2.2 fusion.54
  339.8 2.4 fusion.85
  342.2 2.1 fusion.46
  344.4 2.3 subtract_bitcast_fusion.2
  346.7 2.3 add_bitcast_fusion.2
  349.0 0.5 pad_maximum_fusion.1
  349.5 4.4 copy.108
  353.9 5.3 all-to-all-start.2
  359.3 91.9 %all-to-all-done.2 = f32[2,128,32,128]{3,2,0,1:T(8,128)} async-done(((f32[2,128,32,128]{3,2,0,1:T(8,128)}), f32[2,128,32,128]{3,2,0,1:T(8,128)}, u32[]{:S(2)}, u32[]{:S(2)}) %all-to-all-start.2) | async-done | bytes 4194336 | tf_op jit(solution)/shard_map/all_to_all | solution.py:93
  451.2 2.8 copy.167
  454.0 0.8 fusion.278
  454.8 2.1 fusion.51
  457.0 2.2 fusion.82
  459.1 2.8 bitcast_multiply_fusion.1
  462.0 2.2 fusion.48
  464.2 2.2 fusion.80
  466.3 3.0 bitcast_multiply_fusion
  469.3 2.2 subtract_bitcast_fusion.1
  471.5 2.2 add_bitcast_fusion.1
  473.6 0.5 pad_maximum_fusion.2
  474.1 4.4 copy.110
  478.6 5.2 all-to-all-start.3
  484.7 0.8 copy.123
  485.5 90.7 %all-to-all-done.3 = f32[2,32,128,128]{3,1,0,2:T(8,128)} async-done(((f32[2,32,128,128]{3,1,0,2:T(8,128)}), f32[2,32,128,128]{3,1,0,2:T(8,128)}, u32[]{:S(2)}, u32[]{:S(2)}) %all-to-all-start.3) | async-done | bytes 4194336 | tf_op jit(solution)/shard_map/all_to_all | solution.py:103
  576.2 4.6 copy.111
  580.9 0.8 fusion.277
  582.1 2.2 fusion.12
  584.3 2.2 fusion.14
  586.5 2.2 fusion.32
  588.8 2.5 fusion.29
  591.2 0.6 fusion.40
  591.9 1.3 fusion.28
  (22 shorter events, 1.9 us)
Async XLA Ops:
  59.7 99.7 %all-to-all-start = ((f32[2,32,128,128]{3,1,0,2:T(8,128)}), f32[2,32,128,128]{3,1,0,2:T(8,128)}, u32[]{:S(2)}, u32[]{:S(2)}) async-start(f32[2,32,128,128]{3,1,0,2:T(8,128)} %copy.102), calls=%async_computation | async-start | bytes 8388608 | tf_op jit(solution)/shard_map/all_to_all | solution.py:78
  72.6 92.2 %copy-start.5 = (f32[2]{0:T(128)S(1)}, f32[2]{0:T(128)}, u32[]{:S(2)}) copy-start(f32[2]{0:T(128)} %param.6) | copy-start | bytes 28
  159.4 97.5 %all-to-all-start.1 = ((f32[2,32,128,128]{3,1,0,2:T(8,128)}), f32[2,32,128,128]{3,1,0,2:T(8,128)}, u32[]{:S(2)}, u32[]{:S(2)}) async-start(f32[2,32,128,128]{3,1,0,2:T(8,128)} %copy.104), calls=%async_computation.1 | async-start | bytes 8388608 | tf_op jit(solution)/shard_map/all_to_all | solution.py:78
  164.3 169.7 %all-reduce.2.cloned.1.call-start = ((), (), s32[]{:S(2)}) async-start(), calls=%async_computation.4 | async-start | bytes 4194304 | tf_op jit(solution)/shard_map/psum | solution.py:86
  262.5 4.4 copy-start.3
  264.7 2.2 copy-start.1
  264.7 2.2 copy-start.2
  339.8 2.4 copy-start
  353.9 97.3 %all-to-all-start.2 = ((f32[2,128,32,128]{3,2,0,1:T(8,128)}), f32[2,128,32,128]{3,2,0,1:T(8,128)}, u32[]{:S(2)}, u32[]{:S(2)}) async-start(f32[2,128,32,128]{3,2,0,1:T(8,128)} %copy.108), calls=%async_computation.2 | async-start | bytes 8388608 | tf_op jit(solution)/shard_map/all_to_all | solution.py:93
  478.6 5.7 copy-start.4
  478.6 97.7 %all-to-all-start.3 = ((f32[2,32,128,128]{3,1,0,2:T(8,128)}), f32[2,32,128,128]{3,1,0,2:T(8,128)}, u32[]{:S(2)}, u32[]{:S(2)}) async-start(f32[2,32,128,128]{3,1,0,2:T(8,128)} %copy.110), calls=%async_computation.3 | async-start | bytes 8388608 | tf_op jit(solution)/shard_map/all_to_all | solution.py:103
Sparse Core Ops, SparseCore 0:
  273.1 60.8 all-reduce.1
where the time goes:
time: 610 us; the launch traced here: 600 us
  waiting for transfers between devices  406 us (67%)
  matrix products  111 us (18%)
  local copies, waits for them, and re-layouts  37.5 us (6%)
  starting transfers between devices  22.1 us (4%)
  between operations  15.1 us (2%)
  other arithmetic  9.39 us (2%)
    all_to_all x2, waiting for transfers between devices, local(): lax.all_to_all(stacked[member], 'slab', split_axis=2, concat_axis=1, tile...  162 us
    dot_general x36, matrix products, project(): return jnp.einsum(pattern, values, matrix, precision=lax.Precision.HIGHEST)  111 us
    all_to_all x1, waiting for transfers between devices, local(): lax.all_to_all(jnp.stack((line_real, line_imag)), 'slab', split_axis=1, c...  91.9 us
    all_to_all x1, waiting for transfers between devices, local(): lax.all_to_all(jnp.stack((line_real, line_imag)), 'slab', split_axis=2, c...  90.7 us
    psum x1, waiting for transfers between devices, local(): density = lax.psum(partial_value, 'band')  61 us
  transfers between devices with their start and end apart: 5, of which 5 were waited for; matrix products, arithmetic and copies ran while one was open for 4% of the time, Pallas kernels for 0%

commit v1 on v0

--- a/solution.py
+++ b/solution.py
@@ -2,7 +2,11 @@
 
 import jax
 import jax.numpy as jnp
+import ml_dtypes
+import numpy as np
 from jax import lax
+from jax.experimental import pallas as pl
+from jax.experimental.pallas import tpu as pltpu
 from jax.sharding import PartitionSpec as P
 
 grid_spacing = 0.59
@@ -116,9 +120,255 @@
     return (hartree, xc_potential)
 
 
+def split(values):
+    high = values.astype(jnp.bfloat16)
+    low = (values - high.astype(jnp.float32)).astype(jnp.bfloat16)
+    return high, low
+
+
+def np_split(table):
+    table = np.asarray(table, np.float32)
+    high = table.astype(ml_dtypes.bfloat16)
+    low = (table - high.astype(np.float32)).astype(ml_dtypes.bfloat16)
+    return high, low
+
+
+def np_phases(rows, columns, extent):
+    angle = (np.outer(rows, columns) % extent) * (2.0 * np.pi / extent)
+    return np.cos(angle), np.sin(angle)
+
+
+def column_kernel(low_ref, high_ref, mask_ref, table_ref, out_ref):
+    bands, _, rows = low_ref.shape[:3]
+    for row in range(rows):
+        parts = []
+        for band in range(bands):
+            pair = []
+            for c in range(2):
+                pair.append(
+                    jnp.concatenate([low_ref[band, c, row], high_ref[band, c, row]], axis=0)
+                )
+            parts.append(pair)
+        straight = jnp.concatenate([part for pair in parts for part in pair], axis=0)
+        turned = jnp.concatenate([part for pair in parts for part in (-pair[1], pair[0])], axis=0)
+        both = jnp.concatenate([straight, turned], axis=1)
+        high, low = split(both)
+        stacked = jnp.concatenate([high, low, high], axis=1)
+        result = lax.dot_general(
+            table_ref[...], stacked, (((1,), (1,)), ((), ())), preferred_element_type=jnp.float32
+        )
+        out_ref[:, row, :] = result * mask_ref[row : row + 1, :]
+
+
+def transform_columns(wave_coeffs, lane_mask, extent):
+    bands, _, rows = wave_coeffs.shape[:3]
+    quarter = extent // 4
+    lanes = bands * 2 * 2 * quarter
+    indices = np.arange(extent)
+    cosine, sine = np_phases(indices, indices, extent)
+    high, low = np_split(np.concatenate([cosine, sine], axis=1))
+    table = jnp.asarray(np.concatenate([high, high, low], axis=1))
+    step = 8
+    return pl.pallas_call(
+        column_kernel,
+        grid=(rows // step,),
+        in_specs=[
+            pl.BlockSpec((bands, 2, step, quarter, extent), lambda i: (0, 0, i, 0, 0)),
+            pl.BlockSpec((bands, 2, step, quarter, extent), lambda i: (0, 0, i, 3, 0)),
+            pl.BlockSpec((step, lanes), lambda i: (i, 0)),
+            pl.BlockSpec((extent, 6 * extent), lambda i: (0, 0)),
+        ],
+        out_specs=pl.BlockSpec((extent, step, lanes), lambda i: (0, i, 0)),
+        out_shape=jax.ShapeDtypeStruct((extent, rows, lanes), jnp.float32),
+        compiler_params=pltpu.CompilerParams(vmem_limit_bytes=40 << 20),
+        cost_estimate=pl.CostEstimate(
+            flops=2 * rows * extent * lanes * 6 * extent,
+            bytes_accessed=2 * 4 * extent * rows * lanes,
+            transcendentals=0,
+        ),
+    )(wave_coeffs, wave_coeffs, lane_mask, table)
+
+
+def plane_kernel(first_ref, last_ref, extra_ref, line_ref, weight_ref, left_ref, right_ref, out_ref):
+    extent = out_ref.shape[-1]
+    for plane in range(out_ref.shape[0]):
+        rows = jnp.concatenate([first_ref[plane], last_ref[plane], extra_ref[plane]], axis=0)
+        high, low = split(rows)
+        turned = jnp.dot(
+            left_ref[...],
+            jnp.concatenate([high, low, high], axis=0),
+            preferred_element_type=jnp.float32,
+        )
+        wide = jnp.concatenate([turned[:extent], turned[extent:]], axis=1)
+        high, low = split(wide)
+        psi = jnp.dot(
+            jnp.concatenate([high, low, high], axis=1),
+            right_ref[...],
+            preferred_element_type=jnp.float32,
+        )
+        psi = psi + line_ref[plane]
+        square = psi * psi * weight_ref[...]
+        total = square[:, :extent]
+        for part in range(1, square.shape[1] // extent):
+            total = total + square[:, part * extent : (part + 1) * extent]
+        out_ref[plane] = total
+
+
+def plane_tables(bands, extent):
+    quarter = extent // 4
+    indices = np.arange(extent)
+    kept = np.concatenate([np.arange(quarter), np.arange(3 * quarter, extent)])
+    count = 2 * quarter
+    cosine, sine = np_phases(indices, np.concatenate([kept, [quarter]]), extent)
+    left = np.zeros((2 * extent, count + 16))
+    left[:extent, : count + 1] = cosine
+    left[extent:, : count + 1] = sine
+    high, low = np_split(left)
+    left = np.concatenate([high, high, low], axis=1)
+    cosine, sine = np_phases(kept, indices, extent)
+    lanes = bands * 2 * count
+    right = np.zeros((2, bands, 2, count, bands, 2, extent))
+    for band in range(bands):
+        right[0, band, 0, :, band, 0] = cosine
+        right[0, band, 1, :, band, 0] = -sine
+        right[1, band, 0, :, band, 0] = -sine
+        right[1, band, 1, :, band, 0] = -cosine
+        right[0, band, 0, :, band, 1] = sine
+        right[0, band, 1, :, band, 1] = cosine
+        right[1, band, 0, :, band, 1] = cosine
+        right[1, band, 1, :, band, 1] = -sine
+    high, low = np_split(right.reshape(2 * lanes, bands * 2 * extent))
+    right = np.concatenate([high, high, low], axis=0)
+    return jnp.asarray(left), jnp.asarray(right)
+
+
+def partial_density(first, last, extra, line, weight, extent):
+    planes, rows, lanes = first.shape
+    bands = line.shape[2] // (2 * extent)
+    left, right = plane_tables(bands, extent)
+    step = 4
+    return pl.pallas_call(
+        plane_kernel,
+        grid=(planes // step,),
+        in_specs=[
+            pl.BlockSpec((step, rows, lanes), lambda i: (i, 0, 0)),
+            pl.BlockSpec((step, rows, lanes), lambda i: (i, 0, 0)),
+            pl.BlockSpec((step, 16, lanes), lambda i: (i, 0, 0)),
+            pl.BlockSpec((step, 1, line.shape[2]), lambda i: (i, 0, 0)),
+            pl.BlockSpec((1, line.shape[2]), lambda i: (0, 0)),
+            pl.BlockSpec(left.shape, lambda i: (0, 0)),
+            pl.BlockSpec(right.shape, lambda i: (0, 0)),
+        ],
+        out_specs=pl.BlockSpec((step, extent, extent), lambda i: (i, 0, 0)),
+        out_shape=jax.ShapeDtypeStruct((planes, extent, extent), jnp.float32),
+        compiler_params=pltpu.CompilerParams(vmem_limit_bytes=40 << 20),
+        cost_estimate=pl.CostEstimate(
+            flops=2 * planes * extent * right.shape[0] * right.shape[1],
+            bytes_accessed=4 * planes * (2 * rows * lanes + extent * extent),
+            transcendentals=0,
+        ),
+    )(first, last, extra, line, weight, left, right)
+
+
+def exchange(columns, slab_index, planes):
+    def chunk(index):
+        return lax.dynamic_slice_in_dim(columns, index * planes, planes, 0)
+
+    low_end = slab_index < 2
+    far = lax.ppermute(chunk(jnp.where(low_end, 3, 0)), "slab", [(0, 3), (3, 0)])
+    near = lax.ppermute(chunk(jnp.where(low_end, 1, 2)), "slab", [(0, 1), (3, 2)])
+    middle = lax.ppermute(chunk(jnp.where(low_end, 2, 1)), "slab", [(0, 2), (3, 1)])
+    own = chunk(slab_index)
+    first = lax.select_n(slab_index, own, near, middle, far)
+    last = lax.select_n(slab_index, far, middle, near, own)
+    return first, last
+
+
+def potential(density, extent, kernel_axes):
+    size = lax.axis_size(kernel_axes)
+    member = lax.axis_index(kernel_axes)
+    band_count, slab_count = lax.axis_size("band"), lax.axis_size("slab")
+    rows, columns = density.shape[:2]
+    half = extent // 2 + 1
+    each = -(-half // size)
+    frequencies = np.arange(each * size)
+    cosine, sine = np_phases(frequencies, np.arange(extent), extent)
+    inside = (frequencies < half)[:, None]
+    table = np.stack([cosine * inside, -sine * inside]).reshape(2, size, each, extent)
+    forward = table.transpose(1, 0, 2, 3).reshape(-1, extent)
+    weights = np.where((frequencies == 0) | (frequencies == extent // 2), 1.0, 2.0)
+    backward = forward * np.tile(weights.reshape(size, 1, each), (1, 2, 1)).reshape(-1, 1)
+    backward = backward / float(extent) ** 3
+    forward = jnp.asarray(forward, jnp.float32)
+    backward = jnp.asarray(backward, jnp.float32)
+    lines = project("kz,pz->kp", forward, density.reshape(rows * columns, extent))
+    planes = lax.all_to_all(lines, kernel_axes, split_axis=0, concat_axis=0, tiled=True)
+    planes = planes.reshape(band_count, slab_count, 2 * each, rows, columns)
+    planes = planes.transpose(2, 0, 3, 1, 4).reshape(2, each, extent, extent)
+    cosine_table, sine_table = dft_tables(extent)
+    real_part, imag_part = planes[0], planes[1]
+    real_part, imag_part = rotate(real_part, imag_part, "kxy,yw->kxw", cosine_table, sine_table, -1.0)
+    real_part, imag_part = rotate(real_part, imag_part, "kxy,xw->kwy", cosine_table, sine_table, -1.0)
+    kernel = kernel_block(extent, (member * each, 0, 0), (each, extent, extent))
+    real_part, imag_part = kernel * real_part, kernel * imag_part
+    real_part, imag_part = rotate(real_part, imag_part, "kxy,xw->kwy", cosine_table, sine_table, 1.0)
+    real_part, imag_part = rotate(real_part, imag_part, "kxy,yw->kxw", cosine_table, sine_table, 1.0)
+    planes = jnp.stack((real_part, imag_part)).reshape(
+        2 * each, band_count, rows, slab_count, columns
+    )
+    planes = planes.transpose(1, 3, 0, 2, 4).reshape(-1, rows * columns)
+    lines = lax.all_to_all(planes, kernel_axes, split_axis=0, concat_axis=0, tiled=True)
+    return project("kp,kz->pz", lines, backward).reshape(rows, columns, extent)
+
+
+def quartered(wave_coeffs, column_mask, occupations, core_density):
+    bands, _, rows, extent = wave_coeffs.shape[:4]
+    quarter = extent // 4
+    slab_index = lax.axis_index("slab")
+    mask_rows = lax.dynamic_slice_in_dim(column_mask, slab_index * rows, rows, 0).astype(jnp.float32)
+    kept = jnp.concatenate([mask_rows[:, :quarter], mask_rows[:, 3 * quarter :]], axis=1)
+    lane_mask = jnp.tile(kept, (1, 2 * bands))
+    columns = transform_columns(wave_coeffs, lane_mask, extent)
+    first, last = exchange(columns, slab_index, rows)
+
+    cosine_table, sine_table = dft_tables(extent)
+    single = jnp.stack((wave_coeffs[:, :, 0, quarter], wave_coeffs[:, :, 0, 0]))
+    single = single * jnp.stack(
+        (
+            jnp.where(slab_index == 0, column_mask[0, quarter], 0),
+            jnp.where(slab_index == 1, column_mask[quarter, 0], 0),
+        )
+    ).astype(jnp.float32)[:, None, None, None]
+    single = lax.psum(single, "slab")
+    cosine_part = lax.dynamic_slice_in_dim(cosine_table, slab_index * rows, rows, 0)
+    sine_part = lax.dynamic_slice_in_dim(sine_table, slab_index * rows, rows, 0)
+    single_real, single_imag = rotate(
+        single[:, :, 0], single[:, :, 1], "kbz,wz->kbw", cosine_part, sine_part, 1.0
+    )
+    phase_real, phase_imag = cosine_table[quarter], sine_table[quarter]
+    line_real = single_real[0, ..., None] * phase_real - single_imag[0, ..., None] * phase_imag
+    line_imag = single_real[0, ..., None] * phase_imag + single_imag[0, ..., None] * phase_real
+    line = jnp.stack((line_real, line_imag), axis=1).transpose(2, 0, 1, 3)
+    line = line.reshape(rows, 1, bands * 2 * extent)
+    spot = jnp.stack((single_real[1], single_imag[1]), axis=1).transpose(2, 0, 1)
+    extra = jnp.pad(spot[:, None, :, :, None], ((0, 0), (0, 15), (0, 0), (0, 0), (0, 2 * quarter - 1)))
+    extra = extra.reshape(rows, 16, bands * 4 * quarter)
+    bands_all = lax.axis_size("band") * bands
+    weight = jnp.repeat(occupations / (float(extent) ** 3 * bands_all), 2 * extent)[None]
+    partial = partial_density(first, last, extra, line, weight, extent)
+    summed = lax.psum_scatter(partial, "band", scatter_dimension=1, tiled=True)
+    turned = summed.transpose(2, 0, 1)
+    turned = lax.all_to_all(turned, "slab", split_axis=0, concat_axis=1, tiled=True)
+    density = turned.transpose(2, 0, 1)
+    xc_potential = exchange_correlation(density + core_density)
+    hartree = potential(density, extent, ("band", "slab"))
+    return (hartree, xc_potential)
+
+
 def solution(mesh):
+    body = quartered if mesh.shape["slab"] == 4 else local
     return jax.shard_map(
-        local,
+        body,
         mesh=mesh,
         in_specs=(P("band", None, "slab", None, None), P(), P("band"), P("band", "slab", None)),
         out_specs=(P("band", "slab", None), P("band", "slab", None)),

time: 610 us -> 238 us (0.39); the launches traced: 600 us -> 236 us
  waiting for transfers between devices: 406 us -> 67.1 us
  matrix products: 111 us -> 11.7 us
  blocking collectives: 0 us -> 76.2 us
  Pallas kernels: 0 us -> 19 us
  local copies, waits for them, and re-layouts: 37.5 us -> 20.8 us
    all_to_all x4 -> x2, waiting for transfers between devices: 345 us -> 27.4 us  [the longest x1 14.1 us: potential(): lax.all_to_all(lines, kernel_axes, split_axis=0, concat_axis=0, tiled=True)]
    dot_general x36 -> x22, matrix products: 111 us -> 11.7 us  [project(): return jnp.einsum(pattern, values, matrix, precision=lax.Precision.HIGHEST)]
    psum x0 -> x1, blocking collectives: none -> 62.9 us  [quartered(): single = lax.psum(single, 'slab')]
    psum x1 -> x0, waiting for transfers between devices: 61 us -> none  [local(): density = lax.psum(partial_value, 'band')]
    reduce_scatter x0 -> x1, waiting for transfers between devices: none -> 39.7 us  [quartered(): summed = lax.psum_scatter(partial, 'band', scatter_dimension=1, tiled=True)]
    pallas_call x0 -> x2, Pallas kernels: none -> 19 us  [the longest x1 13.3 us: partial_density(): pl.pallas_call(plane_kernel, grid=(planes // step,), in_specs=[pl.BlockSp...]
    all_to_all x4 -> x2, starting transfers between devices: 21.6 us -> 6.96 us  [the longest x1 4.08 us: potential(): lax.all_to_all(planes, kernel_axes, split_axis=0, concat_axis=0, tiled=True)]
    all_to_all x0 -> x1, blocking collectives: none -> 13.3 us  [quartered(): lax.all_to_all(turned, 'slab', split_axis=0, concat_axis=1, tiled=True)]
  transfers between devices with their start and end apart: 5 -> 6, of which waited for: 5 -> 3; matrix products, arithmetic and copies ran while one was open for 4% -> 3% of each run, Pallas kernels for 0% -> 0%
where the time goes in v1:
time: 238 us; the launch traced here: 236 us
  blocking collectives  76.2 us (32%)
  waiting for transfers between devices  67.1 us (28%)
  local copies, waits for them, and re-layouts  20.8 us (9%)
  Pallas kernels  19 us (8%)
  starting transfers between devices  18.8 us (8%)
  between operations  15.9 us (7%)
  matrix products  11.7 us (5%)
  other arithmetic  6.64 us (3%)
    psum x1, blocking collectives, quartered(): single = lax.psum(single, 'slab')  62.9 us
    reduce_scatter x1, waiting for transfers between devices, quartered(): summed = lax.psum_scatter(partial, 'band', scatter_dimension=1, tiled=True)  39.7 us
    all_to_all x1, waiting for transfers between devices, potential(): lax.all_to_all(lines, kernel_axes, split_axis=0, concat_axis=0, tiled=True)  14.1 us
    pallas_call x1, Pallas kernels, partial_density(): pl.pallas_call(plane_kernel, grid=(planes // step,), in_specs=[pl.BlockSp...  13.3 us
    all_to_all x1, waiting for transfers between devices, potential(): lax.all_to_all(planes, kernel_axes, split_axis=0, concat_axis=0, tiled=True)  13.3 us
    all_to_all x1, blocking collectives, quartered(): lax.all_to_all(turned, 'slab', split_axis=0, concat_axis=1, tiled=True)  13.3 us
    dot_general x22, matrix products, project(): return jnp.einsum(pattern, values, matrix, precision=lax.Precision.HIGHEST)  11.7 us
    unnamed x23, local copies, waits for them, and re-layouts  6.36 us
  transfers between devices with their start and end apart: 6, of which 3 were waited for; matrix products, arithmetic and copies ran while one was open for 3% of the time, Pallas kernels for 0%

profile of v1, /device:TPU:0, one launch (start us, length us, event | category | flops | bytes accessed | tf_op | source)
XLA Modules:
  0.0 236.2 jit_solution(5727261060561555187)
XLA Ops:
  7.2 0.7 dynamic-slice_convert_fusion
  8.2 3.4 %copy-done = f32[2,2,32,128,128]{4,3,2,1,0:T(8,128)S(1)} copy-done((f32[2,2,32,128,128]{4,3,2,1,0:T(8,128)S(1)}, f32[2,2,32,128,128]{4,3,2,1,0:T(8,128)}, u32[]{:S(2)}) %copy-start) | copy-done | bytes 8388632
  11.6 0.9 copy-done.2
  12.5 5.7 %shard_map.104 = f32[128,32,256]{2,1,0:T(8,128)S(1)} custom-call(f32[2,2,32,128,128]{4,3,2,1,0:T(8,128)S(1)} %copy-done, f32[2,2,32,128,128]{4,3,2,1,0:T(8,128)S(1)} %copy-done, f32[32,256]{1,0:T(8,128)S(1)} %tile.10.mask_ref, bf16[128,768]{1,0:T(8,128)(2,1)S(1)} %copy-done.2), custom_call_target="tpu_custom_call" | custom-call | flops 1610612736 | bytes 8388608 | tf_op jit(solution)/shard_map/pallas_call | solution.py:172
  18.3 2.0 constant_dynamic-slice_fusion.2
  20.3 1.0 copy-done.1
  21.3 5.1 %collective-permute-start = (f32[32,32,256]{2,1,0:T(8,128)}, f32[32,32,256]{2,1,0:T(8,128)S(1)}, u32[]{:S(2)}, u32[]{:S(2)}) collective-permute-start(f32[32,32,256]{2,1,0:T(8,128)} %get-tuple-element.6), channel_id=1, source_target_pairs={{0,1},{3,2},{4,5},{7,6},{8,9},{11,10},{12,13},{15,14},{16,17},{19,... | collective-permute-start | bytes 3145736 | tf_op jit(solution)/shard_map/ppermute | solution.py:279
  26.4 3.2 %collective-permute-start.1 = (f32[32,32,256]{2,1,0:T(8,128)}, f32[32,32,256]{2,1,0:T(8,128)}, u32[]{:S(2)}, u32[]{:S(2)}) collective-permute-start(f32[32,32,256]{2,1,0:T(8,128)} %get-tuple-element.8), channel_id=1, source_target_pairs={{0,2},{3,1},{4,6},{7,5},{8,10},{11,9},{12,14},{15,13},{16,18},{19,... | collective-permute-start | bytes 3145736 | tf_op jit(solution)/shard_map/ppermute | solution.py:280
  29.7 3.4 %collective-permute-start.2 = (f32[32,32,256]{2,1,0:T(8,128)}, f32[32,32,256]{2,1,0:T(8,128)}, u32[]{:S(2)}, u32[]{:S(2)}) collective-permute-start(f32[32,32,256]{2,1,0:T(8,128)} %get-tuple-element.7), channel_id=1, source_target_pairs={{0,3},{3,0},{4,7},{7,4},{8,11},{11,8},{12,15},{15,12},{16,19},{19,... | collective-permute-start | bytes 3145736 | tf_op jit(solution)/shard_map/ppermute | solution.py:278
  33.1 1.3 fusion.149
  34.4 0.7 fusion.147
  35.1 0.3 fusion.46
  35.4 0.3 fusion.45
  37.1 62.9 %psum.7 = f32[2,2,2,128]{3,1,0,2:T(2,128)S(1)} all-reduce(f32[2,2,2,128]{3,1,0,2:T(2,128)S(1)} %maximum_multiply_fusion), channel_id=1, replica_groups=mesh['band'=8,'slab'=4] {'slab'}, use_global_device_ids=true, to_apply=%region_0.1 | all-reduce | flops 1024 | bytes 8192 | tf_op jit(solution)/shard_map/psum | solution.py:342
  100.2 0.2 fusion.63
  100.3 0.2 convolution_subtract_fusion.2
  100.9 0.5 pad.4.clone
  101.3 0.8 reshape.160.extra_ref
  102.5 2.5 %select_select_fusion = (f32[32,32,256]{2,1,0:T(8,128)S(1)}, f32[32,32,256]{2,1,0:T(8,128)S(1)}) fusion(f32[32,32,256]{2,1,0:T(8,128)S(1)} %collective-permute-done, f32[32,32,256]{2,1,0:T(8,128)} %collective-permute-done.2, f32[32,32,256]{2,1,0:T(8,128)} %collective-permute-done.1, f32[128,32,256]{2,1,0:T(8,128)} %copy-done.1, s32[]{:T(128)S(6)} %select_n.165, ...), kind=kLoop, calls=%fused_computation.23 | loop fusion | flops 1572864 | bytes 6291463 | tf_op jit(solution)/shard_map/select_n | solution.py:283
  105.0 13.3 %shard_map.105 = f32[32,128,128]{2,1,0:T(8,128)} custom-call(f32[32,32,256]{2,1,0:T(8,128)S(1)} %get-tuple-element.5.first_ref, f32[32,32,256]{2,1,0:T(8,128)S(1)} %get-tuple-element.4.last_ref, f32[32,16,256]{2,1,0:T(8,128)S(1)} %reshape.160.extra_ref, f32[32,1,512]{2,1,0:T(1,128)S(1)} %bitcast.159, f32[1,512]{1,0:T(1,128)S(1)} %bitcast.160, ...), custom_call_target="tpu_custom_call" | custom-call | flops 6442450944 | bytes 4194304 | tf_op jit(solution)/shard_map/pallas_call | solution.py:250
  118.4 39.7 %reduce-scatter.2.cloned.1.call-done = f32[32,16,128]{2,1,0:T(8,128)} async-done(((f32[32,128,128]{2,1,0:T(8,128)}), f32[32,16,128]{2,1,0:T(8,128)}) %reduce-scatter.2.cloned.1.call-update) | async-done | bytes 262160 | tf_op jit(solution)/shard_map/reduce_scatter | solution.py:359
  158.1 1.5 copy.97
  159.5 0.5 reshape.178
  160.0 13.3 %all_to_all.39 = f32[4,1,16384]{2,1,0:T(1,128)S(1)} all-to-all(f32[4,1,16384]{2,1,0:T(1,128)S(1)} %reshape.178), channel_id=1, replica_groups=mesh['band'=8,'slab'=4] {'slab'}, dimensions={0} | all-to-all | bytes 524288 | tf_op jit(solution)/shard_map/all_to_all | solution.py:361
  173.3 0.5 broadcast.345
  173.8 1.4 reduce
  175.2 0.3 reshape.179
  175.5 0.7 copy.98
  176.2 0.5 all_to_all.30
  176.7 0.5 fusion.151
  177.2 0.9 all_to_all.31
  178.0 2.9 %all-to-all-start.1 = ((f32[32,6,512]{2,1,0:T(8,128)}), f32[32,6,512]{2,1,0:T(8,128)S(1)}, u32[]{:S(2)}, u32[]{:S(2)}) async-start(f32[32,6,512]{2,1,0:T(8,128)} %all_to_all.31), calls=%async_computation.2 | async-start | bytes 1048576 | tf_op jit(solution)/shard_map/all_to_all | solution.py:305
  181.0 14.1 %all-to-all-done.1 = f32[32,6,512]{2,1,0:T(8,128)S(1)} async-done(((f32[32,6,512]{2,1,0:T(8,128)}), f32[32,6,512]{2,1,0:T(8,128)S(1)}, u32[]{:S(2)}, u32[]{:S(2)}) %all-to-all-start.1) | async-done | bytes 393248 | tf_op jit(solution)/shard_map/all_to_all | solution.py:305
  195.1 0.2 copy.99
  195.3 0.4 reshape.163
  195.8 0.2 fusion.148
  195.9 0.3 copy.100
  196.3 0.4 squeeze.22
  196.6 0.6 convolution_multiply_fusion.2
  197.2 0.6 fusion.36
  197.8 0.3 copy.101
  198.1 0.4 squeeze.23
  198.4 0.6 fusion.9
  199.0 0.6 convolution_multiply_fusion
  199.6 0.6 fusion.38
  200.2 0.6 convolution_add_fusion.3
  200.8 0.6 fusion.8
  201.4 0.6 fusion.20
  202.0 0.6 fusion.40
  202.6 0.6 fusion.5
  203.2 0.6 fusion.3
  203.8 0.6 fusion.33
  204.4 0.6 fusion.25
  205.0 0.6 fusion.2
  205.6 0.6 fusion.1
  206.2 0.6 fusion
  206.8 0.7 reshape.164
  207.6 0.6 all_to_all.33
  208.2 1.0 copy.111
  209.3 4.1 %all-to-all-start.2 = ((f32[32,6,512]{2,1,0:T(8,128)}), f32[32,6,512]{2,1,0:T(8,128)S(1)}, u32[]{:S(2)}, u32[]{:S(2)}) async-start(f32[32,6,512]{2,1,0:T(8,128)} %copy.111), calls=%async_computation.3 | async-start | bytes 1048576 | tf_op jit(solution)/shard_map/all_to_all | solution.py:320
  213.4 1.0 fusion.12
  214.4 13.3 %all-to-all-done.2 = f32[32,6,512]{2,1,0:T(8,128)S(1)} async-done(((f32[32,6,512]{2,1,0:T(8,128)}), f32[32,6,512]{2,1,0:T(8,128)S(1)}, u32[]{:S(2)}, u32[]{:S(2)}) %all-to-all-start.2) | async-done | bytes 393248 | tf_op jit(solution)/shard_map/all_to_all | solution.py:320
  227.8 0.2 copy.112
  228.0 1.3 fusion.152
  (47 shorter events, 1.5 us)
Async XLA Ops:
  7.2 150.9 %reduce-scatter.2.cloned.1.call-start = ((), (), s32[]{:S(2)}) async-start(), calls=%async_computation.4 | async-start | bytes 2359296 | tf_op jit(solution)/shard_map/reduce_scatter | solution.py:359
  8.2 3.4 %copy-start = (f32[2,2,32,128,128]{4,3,2,1,0:T(8,128)S(1)}, f32[2,2,32,128,128]{4,3,2,1,0:T(8,128)}, u32[]{:S(2)}) copy-start(f32[2,2,32,128,128]{4,3,2,1,0:T(8,128)} %high_ref.1) | copy-start | bytes 25165828
  11.6 0.9 copy-start.2
  18.3 3.0 %copy-start.1 = (f32[128,32,256]{2,1,0:T(8,128)}, f32[128,32,256]{2,1,0:T(8,128)S(1)}, u32[]{:S(2)}) copy-start(f32[128,32,256]{2,1,0:T(8,128)S(1)} %shard_map.104) | copy-start | bytes 12582916
  21.3 81.0 %copy-start.8 = (f32[2]{0:T(128)S(1)}, f32[2]{0:T(128)}, u32[]{:S(2)}) copy-start(f32[2]{0:T(128)} %param.11) | copy-start | bytes 28
  21.3 81.1 %collective-permute-start = (f32[32,32,256]{2,1,0:T(8,128)}, f32[32,32,256]{2,1,0:T(8,128)S(1)}, u32[]{:S(2)}, u32[]{:S(2)}) collective-permute-start(f32[32,32,256]{2,1,0:T(8,128)} %get-tuple-element.6), channel_id=1, source_target_pairs={{0,1},{3,2},{4,5},{7,6},{8,9},{11,10},{12,13},{15,14},{16,17},{19,... | collective-permute-start | bytes 3145736 | tf_op jit(solution)/shard_map/ppermute | solution.py:279
  26.4 76.0 %collective-permute-start.1 = (f32[32,32,256]{2,1,0:T(8,128)}, f32[32,32,256]{2,1,0:T(8,128)}, u32[]{:S(2)}, u32[]{:S(2)}) collective-permute-start(f32[32,32,256]{2,1,0:T(8,128)} %get-tuple-element.8), channel_id=1, source_target_pairs={{0,2},{3,1},{4,6},{7,5},{8,10},{11,9},{12,14},{15,13},{16,18},{19,... | collective-permute-start | bytes 3145736 | tf_op jit(solution)/shard_map/ppermute | solution.py:280
  29.7 72.8 %collective-permute-start.2 = (f32[32,32,256]{2,1,0:T(8,128)}, f32[32,32,256]{2,1,0:T(8,128)}, u32[]{:S(2)}, u32[]{:S(2)}) collective-permute-start(f32[32,32,256]{2,1,0:T(8,128)} %get-tuple-element.7), channel_id=1, source_target_pairs={{0,3},{3,0},{4,7},{7,4},{8,11},{11,8},{12,15},{15,12},{16,19},{19,... | collective-permute-start | bytes 3145736 | tf_op jit(solution)/shard_map/ppermute | solution.py:278
  102.4 2.6 %copy-start.3 = (bf16[1536,512]{1,0:T(8,128)(2,1)S(1)}, bf16[1536,512]{1,0:T(8,128)(2,1)}, u32[]{:S(2)}) copy-start(bf16[1536,512]{1,0:T(8,128)(2,1)} %constant.103.clone.right_ref) | copy-start | bytes 4718596
  102.4 2.6 %copy-start.4 = (bf16[256,240]{1,0:T(8,128)(2,1)S(1)}, bf16[256,240]{1,0:T(8,128)(2,1)}, u32[]{:S(2)}) copy-start(bf16[256,240]{1,0:T(8,128)(2,1)} %constant.102.clone.left_ref) | copy-start | bytes 368644
  175.2 1.5 copy-start.7
  178.0 17.1 %all-to-all-start.1 = ((f32[32,6,512]{2,1,0:T(8,128)}), f32[32,6,512]{2,1,0:T(8,128)S(1)}, u32[]{:S(2)}, u32[]{:S(2)}) async-start(f32[32,6,512]{2,1,0:T(8,128)} %all_to_all.31), calls=%async_computation.2 | async-start | bytes 1048576 | tf_op jit(solution)/shard_map/all_to_all | solution.py:305
  207.6 5.8 %copy-start.5 = (f32[16,32,128]{2,1,0:T(8,128)S(1)}, f32[16,32,128]{2,1,0:T(8,128)}, u32[]{:S(2)}) copy-start(f32[16,32,128]{2,1,0:T(8,128)} %param.12) | copy-start | bytes 786436
  208.2 19.8 %copy-start.6 = (f32[192,128,1]{1,0,2:T(8,128)S(1)}, f32[192,128,1]{1,0,2:T(8,128)}, u32[]{:S(2)}) copy-start(f32[192,128,1]{1,0,2:T(8,128)} %constant.110) | copy-start | bytes 294916
  209.3 18.5 %all-to-all-start.2 = ((f32[32,6,512]{2,1,0:T(8,128)}), f32[32,6,512]{2,1,0:T(8,128)S(1)}, u32[]{:S(2)}, u32[]{:S(2)}) async-start(f32[32,6,512]{2,1,0:T(8,128)} %copy.111), calls=%async_computation.3 | async-start | bytes 1048576 | tf_op jit(solution)/shard_map/all_to_all | solution.py:320
Sparse Core Ops, SparseCore 0:
  118.5 39.5 reduce-scatter.1

commit v2 on v1

--- a/solution.py
+++ b/solution.py
@@ -189,11 +189,148 @@
     )(wave_coeffs, wave_coeffs, lane_mask, table)
 
 
-def plane_kernel(first_ref, last_ref, extra_ref, line_ref, weight_ref, left_ref, right_ref, out_ref):
-    extent = out_ref.shape[-1]
-    for plane in range(out_ref.shape[0]):
-        rows = jnp.concatenate([first_ref[plane], last_ref[plane], extra_ref[plane]], axis=0)
-        high, low = split(rows)
+def density_kernel(
+    columns_ref,
+    lines_ref,
+    weight_ref,
+    left_ref,
+    right_ref,
+    out_ref,
+    land,
+    extra,
+    line,
+    partial,
+    shares,
+    column_send,
+    column_recv,
+    small_send,
+    small_recv,
+    local_sem,
+    share_send,
+    share_recv,
+):
+    mesh_ids = pl.DeviceIdType.MESH
+    planes, rows, extent = out_ref.shape
+    peers = extent // rows
+    pieces = column_recv.shape[1]
+    step = planes // pieces
+    band, slab = lax.axis_index("band"), lax.axis_index("slab")
+
+    barrier = pltpu.get_barrier_semaphore()
+    for shift in range(1, peers):
+        pl.semaphore_signal(
+            barrier, inc=1, device_id=((band + shift) % peers, slab), device_id_type=mesh_ids
+        )
+    for shift in range(1, 4):
+        pl.semaphore_signal(
+            barrier, inc=1, device_id=(band, (slab + shift) % 4), device_id_type=mesh_ids
+        )
+    pl.semaphore_wait(barrier, peers - 1 + 3)
+
+    def column_copy(side, order, target, piece):
+        return pltpu.make_async_remote_copy(
+            src_ref=columns_ref.at[pl.ds(target * planes + piece * step, step)],
+            dst_ref=land.at[side, pl.ds(piece * step, step)],
+            send_sem=column_send.at[order, piece],
+            recv_sem=column_recv.at[side, piece],
+            device_id=(band, target),
+            device_id_type=mesh_ids,
+        )
+
+    def line_copy(order, target):
+        return pltpu.make_async_remote_copy(
+            src_ref=lines_ref.at[pl.ds(target * planes, planes)],
+            dst_ref=line,
+            send_sem=small_send.at[order],
+            recv_sem=small_recv.at[0],
+            device_id=(band, target),
+            device_id_type=mesh_ids,
+        )
+
+    def extra_copy(order, target):
+        return pltpu.make_async_remote_copy(
+            src_ref=columns_ref.at[pl.ds(target * planes, planes), pl.ds(0, 8)],
+            dst_ref=extra,
+            send_sem=small_send.at[order],
+            recv_sem=small_recv.at[1],
+            device_id=(band, target),
+            device_id_type=mesh_ids,
+        )
+
+    def own_columns(side, slab_number):
+        return pltpu.make_async_copy(
+            columns_ref.at[pl.ds(slab_number * planes, planes)], land.at[side], local_sem.at[0]
+        )
+
+    def own_line():
+        return pltpu.make_async_copy(lines_ref.at[pl.ds(0, planes)], line, local_sem.at[1])
+
+    def own_extra():
+        return pltpu.make_async_copy(
+            columns_ref.at[pl.ds(planes, planes), pl.ds(0, 8)], extra, local_sem.at[1]
+        )
+
+    ends = ((0, 0, (3, 2, 1)), (1, 3, (0, 1, 2)))
+
+    @pl.when(slab == 0)
+    def _():
+        for order, target in enumerate((3, 2, 1)):
+            line_copy(order, target).start()
+        own_line().start()
+
+    @pl.when(slab == 1)
+    def _():
+        for order, target in enumerate((0, 2, 3)):
+            extra_copy(order, target).start()
+        own_extra().start()
+
+    for side, number, targets in ends:
+
+        @pl.when(slab == number)
+        def _():
+            for piece in range(pieces):
+                for order, target in enumerate(targets):
+                    column_copy(side, order, target, piece).start()
+            own_columns(side, number).start()
+
+    @pl.when(slab == 0)
+    def _():
+        own_line().wait()
+        own_columns(0, 0).wait()
+
+    @pl.when(slab != 0)
+    def _():
+        line_copy(0, 1).wait_recv()
+
+    @pl.when(slab == 1)
+    def _():
+        own_extra().wait()
+
+    @pl.when(slab != 1)
+    def _():
+        extra_copy(0, 2).wait_recv()
+
+    @pl.when(slab == 3)
+    def _():
+        own_columns(1, 3).wait()
+
+    def share_copy(shift, piece):
+        peer = (band + shift) % peers
+        return pltpu.make_async_remote_copy(
+            src_ref=partial.at[
+                pl.ds(piece * step, step), pl.ds(pl.multiple_of(peer * rows, rows), rows)
+            ],
+            dst_ref=shares.at[shift - 1, pl.ds(piece * step, step)],
+            send_sem=share_send.at[shift - 1, piece],
+            recv_sem=share_recv.at[shift - 1, piece],
+            device_id=(peer, slab),
+            device_id_type=mesh_ids,
+        )
+
+    def transform(plane, carry):
+        filler = jnp.zeros((8, land.shape[3]), jnp.float32)
+        values = jnp.concatenate([land[0, plane], land[1, plane], extra[plane], filler], axis=0)
+        high, low = split(values)
         turned = jnp.dot(
             left_ref[...],
             jnp.concatenate([high, low, high], axis=0),
@@ -206,12 +343,57 @@
             right_ref[...],
             preferred_element_type=jnp.float32,
         )
-        psi = psi + line_ref[plane]
+        psi = psi + line[pl.ds(plane, 1), :]
         square = psi * psi * weight_ref[...]
         total = square[:, :extent]
         for part in range(1, square.shape[1] // extent):
             total = total + square[:, part * extent : (part + 1) * extent]
-        out_ref[plane] = total
+        partial[plane] = total
+        return carry
+
+    for piece in range(pieces):
+
+        @pl.when(slab != 0)
+        def _():
+            column_copy(0, 0, 1, piece).wait_recv()
+
+        @pl.when(slab != 3)
+        def _():
+            column_copy(1, 0, 1, piece).wait_recv()
+
+        lax.fori_loop(piece * step, (piece + 1) * step, transform, 0)
+        for shift in range(1, peers):
+            share_copy(shift, piece).start()
+
+    for piece in range(pieces):
+        section = pl.ds(piece * step, step)
+        own = pl.ds(pl.multiple_of(band * rows, rows), rows)
+        total = partial[section, own, :]
+        for shift in range(1, peers):
+            share_copy(shift, piece).wait_recv()
+            total = total + shares[shift - 1, section]
+        out_ref[section] = total
+
+    for piece in range(pieces):
+        for shift in range(1, peers):
+            share_copy(shift, piece).wait_send()
+    for side, number, targets in ends:
+
+        @pl.when(slab == number)
+        def _():
+            for piece in range(pieces):
+                for order, target in enumerate(targets):
+                    column_copy(side, order, target, piece).wait_send()
+
+    @pl.when(slab == 0)
+    def _():
+        for order, target in enumerate((3, 2, 1)):
+            line_copy(order, target).wait_send()
+
+    @pl.when(slab == 1)
+    def _():
+        for order, target in enumerate((0, 2, 3)):
+            extra_copy(order, target).wait_send()
 
 
 def plane_tables(bands, extent):
@@ -242,46 +424,43 @@
     return jnp.asarray(left), jnp.asarray(right)
 
 
-def partial_density(first, last, extra, line, weight, extent):
-    planes, rows, lanes = first.shape
-    bands = line.shape[2] // (2 * extent)
+def summed_density(columns, lines, weight, extent):
+    _, rows, lanes = columns.shape
+    bands = lines.shape[1] // (2 * extent)
+    planes = extent // 4
+    peers = lax.axis_size("band")
+    share = extent // peers
     left, right = plane_tables(bands, extent)
-    step = 4
+    pieces = 4
+    vmem = pl.BlockSpec(memory_space=pltpu.VMEM)
     return pl.pallas_call(
-        plane_kernel,
-        grid=(planes // step,),
-        in_specs=[
-            pl.BlockSpec((step, rows, lanes), lambda i: (i, 0, 0)),
-            pl.BlockSpec((step, rows, lanes), lambda i: (i, 0, 0)),
-            pl.BlockSpec((step, 16, lanes), lambda i: (i, 0, 0)),
-            pl.BlockSpec((step, 1, line.shape[2]), lambda i: (i, 0, 0)),
-            pl.BlockSpec((1, line.shape[2]), lambda i: (0, 0)),
-            pl.BlockSpec(left.shape, lambda i: (0, 0)),
-            pl.BlockSpec(right.shape, lambda i: (0, 0)),
+        density_kernel,
+        in_specs=[pl.BlockSpec(memory_space=pl.ANY), vmem, vmem, vmem, vmem],
+        out_specs=vmem,
+        out_shape=jax.ShapeDtypeStruct((planes, share, extent), jnp.float32),
+        scratch_shapes=[
+            pltpu.VMEM((2, planes, rows, lanes), jnp.float32),
+            pltpu.VMEM((planes, 8, lanes), jnp.float32),
+            pltpu.VMEM((planes, lines.shape[1]), jnp.float32),
+            pltpu.VMEM((planes, extent, extent), jnp.float32),
+            pltpu.VMEM((peers - 1, planes, share, extent), jnp.float32),
+            pltpu.SemaphoreType.DMA((3, pieces)),
+            pltpu.SemaphoreType.DMA((2, pieces)),
+            pltpu.SemaphoreType.DMA((3,)),
+            pltpu.SemaphoreType.DMA((2,)),
+            pltpu.SemaphoreType.DMA((2,)),
+            pltpu.SemaphoreType.DMA((peers - 1, pieces)),
+            pltpu.SemaphoreType.DMA((peers - 1, pieces)),
         ],
-        out_specs=pl.BlockSpec((step, extent, extent), lambda i: (i, 0, 0)),
-        out_shape=jax.ShapeDtypeStruct((planes, extent, extent), jnp.float32),
-        compiler_params=pltpu.CompilerParams(vmem_limit_bytes=40 << 20),
+        compiler_params=pltpu.CompilerParams(
+            vmem_limit_bytes=40 << 20, collective_id=0, has_side_effects=True
+        ),
         cost_estimate=pl.CostEstimate(
             flops=2 * planes * extent * right.shape[0] * right.shape[1],
             bytes_accessed=4 * planes * (2 * rows * lanes + extent * extent),
             transcendentals=0,
         ),
-    )(first, last, extra, line, weight, left, right)
-
-
-def exchange(columns, slab_index, planes):
-    def chunk(index):
-        return lax.dynamic_slice_in_dim(columns, index * planes, planes, 0)
-
-    low_end = slab_index < 2
-    far = lax.ppermute(chunk(jnp.where(low_end, 3, 0)), "slab", [(0, 3), (3, 0)])
-    near = lax.ppermute(chunk(jnp.where(low_end, 1, 2)), "slab", [(0, 1), (3, 2)])
-    middle = lax.ppermute(chunk(jnp.where(low_end, 2, 1)), "slab", [(0, 2), (3, 1)])
-    own = chunk(slab_index)
-    first = lax.select_n(slab_index, own, near, middle, far)
-    last = lax.select_n(slab_index, far, middle, near, own)
-    return first, last
+    )(columns, lines, weight, left, right)
 
 
 def potential(density, extent, kernel_axes):
@@ -329,34 +508,20 @@
     kept = jnp.concatenate([mask_rows[:, :quarter], mask_rows[:, 3 * quarter :]], axis=1)
     lane_mask = jnp.tile(kept, (1, 2 * bands))
     columns = transform_columns(wave_coeffs, lane_mask, extent)
-    first, last = exchange(columns, slab_index, rows)
-
     cosine_table, sine_table = dft_tables(extent)
-    single = jnp.stack((wave_coeffs[:, :, 0, quarter], wave_coeffs[:, :, 0, 0]))
-    single = single * jnp.stack(
-        (
-            jnp.where(slab_index == 0, column_mask[0, quarter], 0),
-            jnp.where(slab_index == 1, column_mask[quarter, 0], 0),
-        )
-    ).astype(jnp.float32)[:, None, None, None]
-    single = lax.psum(single, "slab")
-    cosine_part = lax.dynamic_slice_in_dim(cosine_table, slab_index * rows, rows, 0)
-    sine_part = lax.dynamic_slice_in_dim(sine_table, slab_index * rows, rows, 0)
+    inside = jnp.where(slab_index == 0, column_mask[0, quarter], 0).astype(jnp.float32)
+    single = wave_coeffs[:, :, 0, quarter] * inside
     single_real, single_imag = rotate(
-        single[:, :, 0], single[:, :, 1], "kbz,wz->kbw", cosine_part, sine_part, 1.0
+        single[:, 0], single[:, 1], "bz,zw->bw", cosine_table, sine_table, 1.0
     )
     phase_real, phase_imag = cosine_table[quarter], sine_table[quarter]
-    line_real = single_real[0, ..., None] * phase_real - single_imag[0, ..., None] * phase_imag
-    line_imag = single_real[0, ..., None] * phase_imag + single_imag[0, ..., None] * phase_real
-    line = jnp.stack((line_real, line_imag), axis=1).transpose(2, 0, 1, 3)
-    line = line.reshape(rows, 1, bands * 2 * extent)
-    spot = jnp.stack((single_real[1], single_imag[1]), axis=1).transpose(2, 0, 1)
-    extra = jnp.pad(spot[:, None, :, :, None], ((0, 0), (0, 15), (0, 0), (0, 0), (0, 2 * quarter - 1)))
-    extra = extra.reshape(rows, 16, bands * 4 * quarter)
+    line_real = single_real[..., None] * phase_real - single_imag[..., None] * phase_imag
+    line_imag = single_real[..., None] * phase_imag + single_imag[..., None] * phase_real
+    lines = jnp.concatenate([line_real, line_imag], axis=2).transpose(1, 0, 2)
+    lines = lines.reshape(extent, bands * 2 * extent)
     bands_all = lax.axis_size("band") * bands
     weight = jnp.repeat(occupations / (float(extent) ** 3 * bands_all), 2 * extent)[None]
-    partial = partial_density(first, last, extra, line, weight, extent)
-    summed = lax.psum_scatter(partial, "band", scatter_dimension=1, tiled=True)
+    summed = summed_density(columns, lines, weight, extent)
     turned = summed.transpose(2, 0, 1)
     turned = lax.all_to_all(turned, "slab", split_axis=0, concat_axis=1, tiled=True)
     density = turned.transpose(2, 0, 1)

time: 238 us -> 176 us (0.74)
  Pallas kernels: 19 us -> 83.3 us
  blocking collectives: 76.2 us -> 23.6 us
  waiting for transfers between devices: 67.1 us -> 27.4 us
  between operations: 15.9 us -> 1.72 us
  starting transfers between devices: 18.8 us -> 7.04 us
  local copies, waits for them, and re-layouts: 20.8 us -> 13.7 us
    pallas_call x1, Pallas kernels: 13.3 us -> 77.6 us  [summed_density(): pl.pallas_call(density_kernel, in_specs=[pl.BlockSpec(memory_space=pl.ANY...]
    psum x1 -> x0, blocking collectives: 62.9 us -> none  [quartered(): single = lax.psum(single, 'slab')]
    reduce_scatter x1 -> x0, waiting for transfers between devices: 39.7 us -> none  [quartered(): summed = lax.psum_scatter(partial, 'band', scatter_dimension=1, tiled=True)]
    ppermute x3 -> x0, starting transfers between devices: 11.8 us -> none  [the longest x1 5.12 us: exchange(): lax.ppermute(chunk(jnp.where(low_end, 1, 2)), 'slab', [(0, 1), (3, 2)])]
    all_to_all x1, blocking collectives: 13.3 us -> 23.6 us  [quartered(): lax.all_to_all(turned, 'slab', split_axis=0, concat_axis=1, tiled=True)]
    select_n x1 -> x0, other arithmetic: 2.53 us -> none  [exchange(): last = lax.select_n(slab_index, far, middle, near, own)]
    unnamed x23 -> x20, local copies, waits for them, and re-layouts: 6.36 us -> 4.3 us
  transfers between devices with their start and end apart: 6 -> 2, of which waited for: 3 -> 2; matrix products, arithmetic and copies ran while one was open for 3% -> 1% of each run, Pallas kernels for 0% -> 0%
where the time goes in v2:
time: 176 us; the launch traced here: 174 us
  Pallas kernels  83.3 us (47%)
  waiting for transfers between devices  27.4 us (16%)
  blocking collectives  23.6 us (13%)
  local copies, waits for them, and re-layouts  13.7 us (8%)
  matrix products  12.7 us (7%)
  starting transfers between devices  7.04 us (4%)
  other arithmetic  4.78 us (3%)
    pallas_call x1, Pallas kernels, summed_density(): pl.pallas_call(density_kernel, in_specs=[pl.BlockSpec(memory_space=pl.ANY...  77.6 us
    all_to_all x1, blocking collectives, quartered(): lax.all_to_all(turned, 'slab', split_axis=0, concat_axis=1, tiled=True)  23.6 us
    all_to_all x1, waiting for transfers between devices, potential(): lax.all_to_all(lines, kernel_axes, split_axis=0, concat_axis=0, tiled=True)  14.1 us
    all_to_all x1, waiting for transfers between devices, potential(): lax.all_to_all(planes, kernel_axes, split_axis=0, concat_axis=0, tiled=True)  13.3 us
    dot_general x22, matrix products, project(): return jnp.einsum(pattern, values, matrix, precision=lax.Precision.HIGHEST)  12.7 us
    pallas_call x1, Pallas kernels, transform_columns(): pl.pallas_call(column_kernel, grid=(rows // step,), in_specs=[pl.BlockSpe...  5.72 us
    unnamed x20, local copies, waits for them, and re-layouts  4.3 us
    all_to_all x1, starting transfers between devices, potential(): lax.all_to_all(planes, kernel_axes, split_axis=0, concat_axis=0, tiled=True)  4.08 us
  transfers between devices with their start and end apart: 2, of which 2 were waited for; matrix products, arithmetic and copies ran while one was open for 1% of the time, Pallas kernels for 0%

profile of v2, /device:TPU:0, one launch (start us, length us, event | category | flops | bytes accessed | tf_op | source)
XLA Modules:
  0.0 174.3 jit_solution(6348394161208088286)
XLA Ops:
  0.7 1.3 slice.39
  2.6 0.7 slice_multiply_fusion
  3.3 0.4 fusion.66
  3.7 0.4 fusion.56
  4.2 0.3 fusion.45
  4.5 0.3 fusion.46
  4.7 0.4 convolution_add_fusion.4
  5.1 0.4 convolution_subtract_fusion.2
  5.5 0.2 multiply_subtract_fusion
  5.8 0.7 dynamic-slice_convert_fusion
  6.5 0.1 fusion.156
  6.6 0.1 pad_maximum_fusion.1
  6.7 0.1 tile.10.mask_ref
  6.8 0.1 broadcast_bitcast_fusion
  6.9 3.4 %copy-done = f32[2,2,32,128,128]{4,3,2,1,0:T(8,128)S(1)} copy-done((f32[2,2,32,128,128]{4,3,2,1,0:T(8,128)S(1)}, f32[2,2,32,128,128]{4,3,2,1,0:T(8,128)}, u32[]{:S(2)}) %copy-start) | copy-done | bytes 8388632
  10.2 5.7 %shard_map.104.columns_ref = f32[128,32,256]{2,1,0:T(8,128)S(1)} custom-call(f32[2,2,32,128,128]{4,3,2,1,0:T(8,128)S(1)} %copy-done, f32[2,2,32,128,128]{4,3,2,1,0:T(8,128)S(1)} %copy-done, f32[32,256]{1,0:T(8,128)S(1)} %tile.10.mask_ref, bf16[128,768]{1,0:T(8,128)(2,1)S(1)} %copy-done.1), custom_call_target="tpu_custom_call" | custom-call | flops 1610612736 | bytes 8388608 | tf_op jit(solution)/shard_map/pallas_call | solution.py:172
  16.0 77.6 %shard_map.105 = f32[32,16,128]{2,1,0:T(8,128)S(1)} custom-call(f32[128,32,256]{2,1,0:T(8,128)S(1)} %shard_map.104.columns_ref, f32[128,512]{1,0:T(8,128)S(1)} %bitcast.130, f32[1,512]{1,0:T(1,128)S(1)} %bitcast.131, bf16[256,240]{1,0:T(8,128)(2,1)S(1)} %copy-done.3, bf16[1536,512]{1,0:T(8,128)(2,1)S(1)} %copy-done.2), custom_call_target="tpu_custom_call" | custom-call | flops 6442450944 | bytes 4194304 | tf_op jit(solution)/shard_map/pallas_call | solution.py:436
  93.6 0.5 copy.77
  94.1 0.5 reshape.139
  94.6 23.6 %all_to_all.39 = f32[4,1,16384]{2,1,0:T(1,128)S(1)} all-to-all(f32[4,1,16384]{2,1,0:T(1,128)S(1)} %reshape.139), channel_id=1, replica_groups=mesh['band'=8,'slab'=4] {'slab'}, dimensions={0} | all-to-all | bytes 524288 | tf_op jit(solution)/shard_map/all_to_all | solution.py:526
  118.2 0.5 broadcast.299
  118.7 1.4 reduce
  120.1 0.3 reshape.140
  120.5 0.0 copy-start.6
  120.5 0.7 copy.78
  121.2 0.5 all_to_all.30
  121.6 0.5 fusion.158
  122.1 0.8 all_to_all.31
  123.0 3.0 %all-to-all-start.1 = ((f32[32,6,512]{2,1,0:T(8,128)}), f32[32,6,512]{2,1,0:T(8,128)S(1)}, u32[]{:S(2)}, u32[]{:S(2)}) async-start(f32[32,6,512]{2,1,0:T(8,128)} %all_to_all.31), calls=%async_computation.1 | async-start | bytes 1048576 | tf_op jit(solution)/shard_map/all_to_all | solution.py:484
  126.0 0.1 broadcast_add_fusion
  126.1 14.1 %all-to-all-done.1 = f32[32,6,512]{2,1,0:T(8,128)S(1)} async-done(((f32[32,6,512]{2,1,0:T(8,128)}), f32[32,6,512]{2,1,0:T(8,128)S(1)}, u32[]{:S(2)}, u32[]{:S(2)}) %all-to-all-start.1) | async-done | bytes 393248 | tf_op jit(solution)/shard_map/all_to_all | solution.py:484
  140.1 0.2 copy.79
  140.4 0.4 reshape.126
  140.8 0.2 fusion.155
  141.0 0.3 copy.80
  141.3 0.4 squeeze.19
  141.6 0.6 convolution_multiply_fusion.2
  142.2 0.6 fusion.36
  142.8 0.3 copy.81
  143.1 0.4 squeeze.20
  143.5 0.6 fusion.9
  144.0 0.6 convolution_multiply_fusion
  144.6 0.6 fusion.38
  145.2 0.6 convolution_add_fusion.3
  145.8 0.6 fusion.8
  146.4 0.6 fusion.20
  147.0 0.6 fusion.40
  147.6 0.6 fusion.5
  148.2 0.6 fusion.3
  148.9 0.6 fusion.33
  149.4 0.6 fusion.25
  150.0 0.6 fusion.2
  150.6 0.6 fusion.1
  151.2 0.6 fusion
  151.8 0.7 reshape.127
  152.5 0.1 copy.112
  152.6 0.6 all_to_all.33
  153.2 1.0 copy.91
  154.3 4.1 %all-to-all-start.2 = ((f32[32,6,512]{2,1,0:T(8,128)}), f32[32,6,512]{2,1,0:T(8,128)S(1)}, u32[]{:S(2)}, u32[]{:S(2)}) async-start(f32[32,6,512]{2,1,0:T(8,128)} %copy.91), calls=%async_computation.2 | async-start | bytes 1048576 | tf_op jit(solution)/shard_map/all_to_all | solution.py:499
  158.4 1.0 fusion.12
  159.4 13.3 %all-to-all-done.2 = f32[32,6,512]{2,1,0:T(8,128)S(1)} async-done(((f32[32,6,512]{2,1,0:T(8,128)}), f32[32,6,512]{2,1,0:T(8,128)S(1)}, u32[]{:S(2)}, u32[]{:S(2)}) %all-to-all-start.2) | async-done | bytes 393248 | tf_op jit(solution)/shard_map/all_to_all | solution.py:499
  172.7 0.1 all_to_all.35
  172.8 0.2 copy.92
  173.0 1.3 fusion.159
  (24 shorter events, 0.2 us)
Async XLA Ops:
  0.6 6.2 %copy-start.1 = (bf16[128,768]{1,0:T(8,128)(2,1)S(1)}, bf16[128,768]{1,0:T(8,128)(2,1)}, u32[]{:S(2)}) copy-start(bf16[128,768]{1,0:T(8,128)(2,1)} %constant.97.clone.table_ref) | copy-start | bytes 589828
  0.6 6.1 %copy-start.7 = (f32[2]{0:T(128)S(1)}, f32[2]{0:T(128)}, u32[]{:S(2)}) copy-start(f32[2]{0:T(128)} %param.11) | copy-start | bytes 28
  6.9 3.4 %copy-start = (f32[2,2,32,128,128]{4,3,2,1,0:T(8,128)S(1)}, f32[2,2,32,128,128]{4,3,2,1,0:T(8,128)}, u32[]{:S(2)}) copy-start(f32[2,2,32,128,128]{4,3,2,1,0:T(8,128)} %high_ref.1) | copy-start | bytes 25165828
  10.2 5.7 %copy-start.2 = (bf16[1536,512]{1,0:T(8,128)(2,1)S(1)}, bf16[1536,512]{1,0:T(8,128)(2,1)}, u32[]{:S(2)}) copy-start(bf16[1536,512]{1,0:T(8,128)(2,1)} %constant.99.clone.right_ref) | copy-start | bytes 4718596
  10.2 5.7 %copy-start.3 = (bf16[256,240]{1,0:T(8,128)(2,1)S(1)}, bf16[256,240]{1,0:T(8,128)(2,1)}, u32[]{:S(2)}) copy-start(bf16[256,240]{1,0:T(8,128)(2,1)} %constant.98.clone.left_ref) | copy-start | bytes 368644
  120.5 1.2 copy-start.6
  123.0 17.2 %all-to-all-start.1 = ((f32[32,6,512]{2,1,0:T(8,128)}), f32[32,6,512]{2,1,0:T(8,128)S(1)}, u32[]{:S(2)}, u32[]{:S(2)}) async-start(f32[32,6,512]{2,1,0:T(8,128)} %all_to_all.31), calls=%async_computation.1 | async-start | bytes 1048576 | tf_op jit(solution)/shard_map/all_to_all | solution.py:484
  152.6 5.8 %copy-start.4 = (f32[16,32,128]{2,1,0:T(8,128)S(1)}, f32[16,32,128]{2,1,0:T(8,128)}, u32[]{:S(2)}) copy-start(f32[16,32,128]{2,1,0:T(8,128)} %param.12) | copy-start | bytes 786436
  154.3 18.5 %all-to-all-start.2 = ((f32[32,6,512]{2,1,0:T(8,128)}), f32[32,6,512]{2,1,0:T(8,128)S(1)}, u32[]{:S(2)}, u32[]{:S(2)}) async-start(f32[32,6,512]{2,1,0:T(8,128)} %copy.91), calls=%async_computation.2 | async-start | bytes 1048576 | tf_op jit(solution)/shard_map/all_to_all | solution.py:499
  158.4 14.6 %copy-start.5 = (f32[192,128,1]{1,0,2:T(8,128)S(1)}, f32[192,128,1]{1,0,2:T(8,128)}, u32[]{:S(2)}) copy-start(f32[192,128,1]{1,0,2:T(8,128)} %constant.104) | copy-start | bytes 294916

commit v3 on v2

--- a/solution.py
+++ b/solution.py
@@ -124,6 +124,12 @@
     high = values.astype(jnp.bfloat16)
     low = (values - high.astype(jnp.float32)).astype(jnp.bfloat16)
     return high, low
+
+
+def full_dot(left, right):
+    return jnp.dot(
+        left, right, precision=lax.Precision.HIGHEST, preferred_element_type=jnp.float32
+    )
 
 
 def np_split(table):
@@ -195,7 +201,13 @@
     weight_ref,
     left_ref,
     right_ref,
-    out_ref,
+    depth_ref,
+    across_ref,
+    across_back_ref,
+    along_ref,
+    along_back_ref,
+    density_ref,
+    final_ref,
     land,
     extra,
     line,
@@ -208,9 +220,25 @@
     local_sem,
     share_send,
     share_recv,
+    gathered,
+    spectrum,
+    rods,
+    rods_out,
+    returned,
+    spread,
+    columns_out,
+    final,
+    gather_send,
+    gather_recv,
+    band_send,
+    band_recv,
+    final_send,
+    final_recv,
 ):
     mesh_ids = pl.DeviceIdType.MESH
-    planes, rows, extent = out_ref.shape
+    planes = line.shape[0]
+    _, rows, extent = gathered.shape
+    per_slab, each = spectrum.shape[1], rods.shape[1]
     peers = extent // rows
     pieces = column_recv.shape[1]
     step = planes // pieces
@@ -351,29 +379,161 @@
         partial[plane] = total
         return carry
 
-    for piece in range(pieces):
-
-        @pl.when(slab != 0)
-        def _():
-            column_copy(0, 0, 1, piece).wait_recv()
-
-        @pl.when(slab != 3)
-        def _():
-            column_copy(1, 0, 1, piece).wait_recv()
-
-        lax.fori_loop(piece * step, (piece + 1) * step, transform, 0)
-        for shift in range(1, peers):
-            share_copy(shift, piece).start()
-
-    for piece in range(pieces):
+    def gather_copy(shift, piece):
+        target = (slab + shift) % 4
+        section = pl.ds(slab * planes + piece * step, step)
+        return pltpu.make_async_remote_copy(
+            src_ref=gathered.at[section],
+            dst_ref=gathered.at[section],
+            send_sem=gather_send.at[shift - 1, piece],
+            recv_sem=gather_recv.at[shift - 1, piece],
+            device_id=(band, target),
+            device_id_type=mesh_ids,
+        )
+
+    def finish_piece(piece):
         section = pl.ds(piece * step, step)
         own = pl.ds(pl.multiple_of(band * rows, rows), rows)
         total = partial[section, own, :]
         for shift in range(1, peers):
             share_copy(shift, piece).wait_recv()
             total = total + shares[shift - 1, section]
-        out_ref[section] = total
-
+        gathered[pl.ds(slab * planes + piece * step, step)] = total
+        for shift in range(1, 4):
+            gather_copy(shift, piece).start()
+
+    for piece in range(pieces):
+
+        @pl.when(slab != 0)
+        def _():
+            column_copy(0, 0, 1, piece).wait_recv()
+
+        @pl.when(slab != 3)
+        def _():
+            column_copy(1, 0, 1, piece).wait_recv()
+
+        lax.fori_loop(piece * step, (piece + 1) * step, transform, 0)
+        for shift in range(1, peers):
+            share_copy(shift, piece).start()
+        if piece > 0:
+            finish_piece(piece - 1)
+    finish_piece(pieces - 1)
+
+    for piece in range(pieces):
+        for shift in range(1, 4):
+            gather_copy(shift, piece).wait_recv()
+
+    table = depth_ref[slab]
+    for row in range(rows):
+        lines = full_dot(table, gathered[:, row, :])
+        returned[0, :, row, :] = lines[:per_slab]
+        returned[1, :, row, :] = lines[per_slab:]
+
+    def side_by_side(source):
+        real_part = source[0].reshape(per_slab * rows, extent)
+        imag_part = source[1].reshape(per_slab * rows, extent)
+        return jnp.concatenate([real_part, imag_part], axis=1)
+
+    result = full_dot(side_by_side(returned), along_ref[...])
+    spectrum[0] = result[:, :extent].reshape(per_slab, rows, extent)
+    spectrum[1] = result[:, extent:].reshape(per_slab, rows, extent)
+
+    own_rows = pl.ds(pl.multiple_of(band * rows, rows), rows)
+
+    def rods_copy(shift):
+        peer = (band + shift) % peers
+        return pltpu.make_async_remote_copy(
+            src_ref=spectrum.at[:, pl.ds(peer * each, each)],
+            dst_ref=rods.at[:, :, own_rows],
+            send_sem=band_send.at[0, shift - 1],
+            recv_sem=band_recv.at[0, shift - 1],
+            device_id=(peer, slab),
+            device_id_type=mesh_ids,
+        )
+
+    def return_copy(shift):
+        peer = (band + shift) % peers
+        return pltpu.make_async_remote_copy(
+            src_ref=rods_out.at[:, :, pl.ds(pl.multiple_of(peer * rows, rows), rows)],
+            dst_ref=spread.at[:, pl.ds(band * each, each)],
+            send_sem=band_send.at[1, shift - 1],
+            recv_sem=band_recv.at[1, shift - 1],
+            device_id=(peer, slab),
+            device_id_type=mesh_ids,
+        )
+
+    for shift in range(1, peers):
+        rods_copy(shift).start()
+    rods[:, :, own_rows, :] = spectrum[:, pl.ds(band * each, each)]
+    density_ref[...] = gathered[...]
+    for shift in range(1, peers):
+        rods_copy(shift).wait_recv()
+
+    def squares(dimension):
+        index = lax.broadcasted_iota(jnp.int32, (extent, extent), dimension)
+        shifted = jnp.where(index >= extent // 2, index - extent, index)
+        return shifted * shifted
+
+    flat = squares(0) + squares(1)
+    length = extent * grid_spacing
+    for item in range(each):
+        stacked = jnp.concatenate([rods[0, item], rods[1, item]], axis=0)
+        lines = full_dot(across_ref[...], stacked)
+        frequency = slab * per_slab + band * each + item
+        squared = flat + frequency * frequency
+        kernel = (length * length / math.pi) / jnp.maximum(squared, 1).astype(jnp.float32)
+        kernel = jnp.where(squared == 0, 0.0, kernel)
+        high, low = split(lines * jnp.concatenate([kernel, kernel], axis=0))
+        lines = jnp.dot(
+            across_back_ref[...],
+            jnp.concatenate([high, low, high], axis=0),
+            preferred_element_type=jnp.float32,
+        )
+        rods_out[0, item] = lines[:extent]
+        rods_out[1, item] = lines[extent:]
+
+    for shift in range(1, peers):
+        return_copy(shift).start()
+    spread[:, pl.ds(band * each, each)] = rods_out[:, :, own_rows, :]
+    for shift in range(1, peers):
+        return_copy(shift).wait_recv()
+
+    high, low = split(side_by_side(spread))
+    result = jnp.dot(
+        jnp.concatenate([high, low, high], axis=1),
+        along_back_ref[...],
+        preferred_element_type=jnp.float32,
+    )
+    half = per_slab * rows
+    for c in range(2):
+        flipped = result[:, c * extent : (c + 1) * extent].T
+        columns_out[:, c * half : (c + 1) * half] = flipped
+
+    def final_copy(shift):
+        target = (slab + shift) % 4
+        return pltpu.make_async_remote_copy(
+            src_ref=columns_out.at[pl.ds(pl.multiple_of(target * planes, planes), planes)],
+            dst_ref=final.at[slab],
+            send_sem=final_send.at[shift - 1],
+            recv_sem=final_recv.at[shift - 1],
+            device_id=(band, target),
+            device_id_type=mesh_ids,
+        )
+
+    for shift in range(1, 4):
+        final_copy(shift).start()
+    final[slab] = columns_out[pl.ds(pl.multiple_of(slab * planes, planes), planes)]
+    for shift in range(1, 4):
+        final_copy(shift).wait_recv()
+    final_ref[...] = final[...]
+
+    for shift in range(1, peers):
+        rods_copy(shift).wait_send()
+        return_copy(shift).wait_send()
+    for shift in range(1, 4):
+        final_copy(shift).wait_send()
+        for piece in range(pieces):
+            gather_copy(shift, piece).wait_send()
     for piece in range(pieces):
         for shift in range(1, peers):
             share_copy(shift, piece).wait_send()
@@ -424,6 +584,34 @@
     return jnp.asarray(left), jnp.asarray(right)
 
 
+def line_tables(extent, slabs, peers):
+    half = extent // 2 + 1
+    per_slab = -(-half // (slabs * peers)) * peers
+    indices = np.arange(extent)
+    frequencies = np.arange(slabs * per_slab)
+    cosine, sine = np_phases(frequencies, indices, extent)
+    inside = (frequencies < half)[:, None]
+    table = np.stack([cosine * inside, -sine * inside]).reshape(2, slabs, per_slab, extent)
+    table = table.transpose(1, 0, 2, 3)
+    counts = np.where((frequencies == 0) | (frequencies == extent // 2), 1.0, 2.0)
+    backward = table * counts.reshape(slabs, 1, per_slab, 1) / float(extent) ** 3
+    depth = table.reshape(slabs, 2 * per_slab, extent)
+    cosine, sine = np_phases(indices, indices, extent)
+    across = np.block([[cosine, sine], [-sine, cosine]])
+    high, low = np_split(across.T)
+    across_back = np.concatenate([high, high, low], axis=1)
+    high, low = np_split(across)
+    along_back = np.concatenate([high, high, low], axis=0)
+    return (
+        jnp.asarray(depth, jnp.float32),
+        jnp.asarray(across, jnp.float32),
+        jnp.asarray(across_back),
+        jnp.asarray(across.T, jnp.float32),
+        jnp.asarray(along_back),
+        jnp.asarray(backward, jnp.float32),
+    )
+
+
 def summed_density(columns, lines, weight, extent):
     _, rows, lanes = columns.shape
     bands = lines.shape[1] // (2 * extent)
@@ -431,13 +619,19 @@
     peers = lax.axis_size("band")
     share = extent // peers
     left, right = plane_tables(bands, extent)
+    *tables, backward = line_tables(extent, 4, peers)
+    per_slab = tables[0].shape[1] // 2
+    each = per_slab // peers
     pieces = 4
     vmem = pl.BlockSpec(memory_space=pltpu.VMEM)
-    return pl.pallas_call(
+    density, final = pl.pallas_call(
         density_kernel,
-        in_specs=[pl.BlockSpec(memory_space=pl.ANY), vmem, vmem, vmem, vmem],
-        out_specs=vmem,
-        out_shape=jax.ShapeDtypeStruct((planes, share, extent), jnp.float32),
+        in_specs=[pl.BlockSpec(memory_space=pl.ANY)] + [vmem] * 9,
+        out_specs=(vmem, vmem),
+        out_shape=(
+            jax.ShapeDtypeStruct((extent, share, extent), jnp.float32),
+            jax.ShapeDtypeStruct((4, planes, 2 * per_slab * share), jnp.float32),
+        ),
         scratch_shapes=[
             pltpu.VMEM((2, planes, rows, lanes), jnp.float32),
             pltpu.VMEM((planes, 8, lanes), jnp.float32),
@@ -451,6 +645,20 @@
             pltpu.SemaphoreType.DMA((2,)),
             pltpu.SemaphoreType.DMA((peers - 1, pieces)),
             pltpu.SemaphoreType.DMA((peers - 1, pieces)),
+            pltpu.VMEM((extent, share, extent), jnp.float32),
+            pltpu.VMEM((2, per_slab, share, extent), jnp.float32),
+            pltpu.VMEM((2, each, extent, extent), jnp.float32),
+            pltpu.VMEM((2, each, extent, extent), jnp.float32),
+            pltpu.VMEM((2, per_slab, share, extent), jnp.float32),
+            pltpu.VMEM((2, per_slab, share, extent), jnp.float32),
+            pltpu.VMEM((extent, 2 * per_slab * share), jnp.float32),
+            pltpu.VMEM((4, planes, 2 * per_slab * share), jnp.float32),
+            pltpu.SemaphoreType.DMA((3, pieces)),
+            pltpu.SemaphoreType.DMA((3, pieces)),
+            pltpu.SemaphoreType.DMA((2, peers - 1)),
+            pltpu.SemaphoreType.DMA((2, peers - 1)),
+            pltpu.SemaphoreType.DMA((3,)),
+            pltpu.SemaphoreType.DMA((3,)),
         ],
         compiler_params=pltpu.CompilerParams(
             vmem_limit_bytes=40 << 20, collective_id=0, has_side_effects=True
@@ -460,44 +668,11 @@
             bytes_accessed=4 * planes * (2 * rows * lanes + extent * extent),
             transcendentals=0,
         ),
-    )(columns, lines, weight, left, right)
-
-
-def potential(density, extent, kernel_axes):
-    size = lax.axis_size(kernel_axes)
-    member = lax.axis_index(kernel_axes)
-    band_count, slab_count = lax.axis_size("band"), lax.axis_size("slab")
-    rows, columns = density.shape[:2]
-    half = extent // 2 + 1
-    each = -(-half // size)
-    frequencies = np.arange(each * size)
-    cosine, sine = np_phases(frequencies, np.arange(extent), extent)
-    inside = (frequencies < half)[:, None]
-    table = np.stack([cosine * inside, -sine * inside]).reshape(2, size, each, extent)
-    forward = table.transpose(1, 0, 2, 3).reshape(-1, extent)
-    weights = np.where((frequencies == 0) | (frequencies == extent // 2), 1.0, 2.0)
-    backward = forward * np.tile(weights.reshape(size, 1, each), (1, 2, 1)).reshape(-1, 1)
-    backward = backward / float(extent) ** 3
-    forward = jnp.asarray(forward, jnp.float32)
-    backward = jnp.asarray(backward, jnp.float32)
-    lines = project("kz,pz->kp", forward, density.reshape(rows * columns, extent))
-    planes = lax.all_to_all(lines, kernel_axes, split_axis=0, concat_axis=0, tiled=True)
-    planes = planes.reshape(band_count, slab_count, 2 * each, rows, columns)
-    planes = planes.transpose(2, 0, 3, 1, 4).reshape(2, each, extent, extent)
-    cosine_table, sine_table = dft_tables(extent)
-    real_part, imag_part = planes[0], planes[1]
-    real_part, imag_part = rotate(real_part, imag_part, "kxy,yw->kxw", cosine_table, sine_table, -1.0)
-    real_part, imag_part = rotate(real_part, imag_part, "kxy,xw->kwy", cosine_table, sine_table, -1.0)
-    kernel = kernel_block(extent, (member * each, 0, 0), (each, extent, extent))
-    real_part, imag_part = kernel * real_part, kernel * imag_part
-    real_part, imag_part = rotate(real_part, imag_part, "kxy,xw->kwy", cosine_table, sine_table, 1.0)
-    real_part, imag_part = rotate(real_part, imag_part, "kxy,yw->kxw", cosine_table, sine_table, 1.0)
-    planes = jnp.stack((real_part, imag_part)).reshape(
-        2 * each, band_count, rows, slab_count, columns
-    )
-    planes = planes.transpose(1, 3, 0, 2, 4).reshape(-1, rows * columns)
-    lines = lax.all_to_all(planes, kernel_axes, split_axis=0, concat_axis=0, tiled=True)
-    return project("kp,kz->pz", lines, backward).reshape(rows, columns, extent)
+    )(columns, lines, weight, left, right, *tables)
+    final = final.reshape(4, planes, 2, per_slab, share)
+    hartree = jnp.einsum("syckx,sckz->xyz", final, backward, precision=lax.Precision.HIGHEST)
+    own = lax.dynamic_slice_in_dim(density, lax.axis_index("slab") * planes, planes, 2)
+    return hartree, own.transpose(1, 2, 0)
 
 
 def quartered(wave_coeffs, column_mask, occupations, core_density):
@@ -521,12 +696,8 @@
     lines = lines.reshape(extent, bands * 2 * extent)
     bands_all = lax.axis_size("band") * bands
     weight = jnp.repeat(occupations / (float(extent) ** 3 * bands_all), 2 * extent)[None]
-    summed = summed_density(columns, lines, weight, extent)
-    turned = summed.transpose(2, 0, 1)
-    turned = lax.all_to_all(turned, "slab", split_axis=0, concat_axis=1, tiled=True)
-    density = turned.transpose(2, 0, 1)
+    hartree, density = summed_density(columns, lines, weight, extent)
     xc_potential = exchange_correlation(density + core_density)
-    hartree = potential(density, extent, ("band", "slab"))
     return (hartree, xc_potential)
 
 

time: 176 us -> 152 us (0.86)
  Pallas kernels: 83.3 us -> 127 us
  waiting for transfers between devices: 27.4 us -> 0 us
  blocking collectives: 23.6 us -> 0 us
  matrix products: 12.7 us -> 3.47 us
  starting transfers between devices: 7.04 us -> 0 us
    pallas_call x1, Pallas kernels: 77.6 us -> 122 us  [summed_density(): pl.pallas_call(density_kernel, in_specs=[pl.BlockSpec(memory_space=pl.ANY...]
    all_to_all x2 -> x0, waiting for transfers between devices: 27.4 us -> none  [the longest x1 14.1 us: potential(): lax.all_to_all(lines, kernel_axes, split_axis=0, concat_axis=0, tiled=True)]
    all_to_all x1 -> x0, blocking collectives: 23.6 us -> none  [quartered(): lax.all_to_all(turned, 'slab', split_axis=0, concat_axis=1, tiled=True)]
    dot_general x22 -> x4, matrix products: 12.7 us -> 1.66 us  [project(): return jnp.einsum(pattern, values, matrix, precision=lax.Precision.HIGHEST)]
    all_to_all x2 -> x0, starting transfers between devices: 7.04 us -> none  [the longest x1 4.08 us: potential(): lax.all_to_all(planes, kernel_axes, split_axis=0, concat_axis=0, tiled=True)]
    all_to_all x8 -> x0, local copies, waits for them, and re-layouts: 4.44 us -> none  [the longest x3 1.71 us: potential(): lax.all_to_all(planes, kernel_axes, split_axis=0, concat_axis=0, tiled=True)]
    unnamed x20 -> x29, local copies, waits for them, and re-layouts: 4.3 us -> 6.79 us
    dot_general x0 -> x1, matrix products: none -> 1.81 us  [summed_density(): jnp.einsum('syckx,sckz->xyz', final, backward, precision=lax.Precision.HI...]
  transfers between devices with their start and end apart: 2 -> 0, of which waited for: 2 -> 0; matrix products, arithmetic and copies ran while one was open for 1% -> 0% of each run, Pallas kernels for 0% -> 0%
where the time goes in v3:
time: 152 us; the launch traced here: 150 us
  Pallas kernels  127 us (84%)
  local copies, waits for them, and re-layouts  13 us (9%)
  other arithmetic  4.8 us (3%)
  matrix products  3.47 us (2%)
    pallas_call x1, Pallas kernels, summed_density(): pl.pallas_call(density_kernel, in_specs=[pl.BlockSpec(memory_space=pl.ANY...  122 us
    unnamed x29, local copies, waits for them, and re-layouts  6.79 us
    pallas_call x1, Pallas kernels, transform_columns(): pl.pallas_call(column_kernel, grid=(rows // step,), in_specs=[pl.BlockSpe...  5.73 us

profile of v3, /device:TPU:0, one launch (start us, length us, event | category | flops | bytes accessed | tf_op | source)
XLA Modules:
  0.0 150.1 jit_solution(5108507316439758825)
XLA Ops:
  0.6 0.0 copy-start.1
  0.6 1.3 slice.31
  2.6 0.7 slice_multiply_fusion
  3.3 0.4 fusion.15
  3.7 0.4 convolution_add_fusion
  4.2 0.4 fusion.13
  4.6 0.4 convolution_subtract_fusion
  5.0 0.3 fusion.10
  5.3 0.3 fusion.11
  5.6 0.1 multiply_subtract_fusion
  5.8 0.7 dynamic-slice_convert_fusion
  6.5 0.1 fusion.34
  6.6 0.1 pad_maximum_fusion
  6.7 0.1 tile.10.mask_ref
  6.8 0.0 copy-done.1
  6.8 0.0 copy-start
  6.8 3.4 %copy-done = f32[2,2,32,128,128]{4,3,2,1,0:T(8,128)S(1)} copy-done((f32[2,2,32,128,128]{4,3,2,1,0:T(8,128)S(1)}, f32[2,2,32,128,128]{4,3,2,1,0:T(8,128)}, u32[]{:S(2)}) %copy-start) | copy-done | bytes 8388632
  10.2 0.0 copy-start.11
  10.2 0.0 copy-start.2
  10.2 0.0 copy-start.3
  10.2 0.0 copy-start.4
  10.2 0.0 copy-start.5
  10.2 0.0 copy-start.6
  10.2 0.0 copy-start.7
  10.2 0.0 copy-start.8
  10.2 5.7 %shard_map.140.columns_ref = f32[128,32,256]{2,1,0:T(8,128)S(1)} custom-call(f32[2,2,32,128,128]{4,3,2,1,0:T(8,128)S(1)} %copy-done, f32[2,2,32,128,128]{4,3,2,1,0:T(8,128)S(1)} %copy-done, f32[32,256]{1,0:T(8,128)S(1)} %tile.10.mask_ref, bf16[128,768]{1,0:T(8,128)(2,1)S(1)} %copy-done.1), custom_call_target="tpu_custom_call" | custom-call | flops 1610612736 | bytes 8388608 | tf_op jit(solution)/shard_map/pallas_call | solution.py:178
  16.0 0.0 copy-done.11
  16.0 0.1 broadcast_bitcast_fusion
  16.1 0.0 copy-done.2
  16.1 0.0 copy-done.3
  16.1 0.0 copy-done.4
  16.1 0.0 copy-done.5
  16.1 0.0 copy-done.6
  16.1 0.0 copy-done.7
  16.1 0.0 copy-done.8
  16.1 0.0 copy-start.9
  16.1 121.6 %shard_map.141 = (f32[128,16,128]{2,1,0:T(8,128)S(1)}, f32[4,32,768]{2,1,0:T(8,128)S(1)}) custom-call(f32[128,32,256]{2,1,0:T(8,128)S(1)} %shard_map.140.columns_ref, f32[128,512]{1,0:T(8,128)S(1)} %bitcast.36, f32[1,512]{1,0:T(1,128)S(1)} %bitcast.37, bf16[256,240]{1,0:T(8,128)(2,1)S(1)} %copy-done.7, bf16[1536,512]{1,0:T(8,128)(2,1)S(1)} %copy-done.2, ...), custom_call_target="tpu_custom_call" | custom-call | flops 6442450944 | bytes 4194304 | tf_op jit(solution)/shard_map/pallas_call | solution.py:627
  137.7 0.0 copy-done.9
  137.7 1.4 copy.31
  139.1 2.6 %fusion.2 = f32[16,32,128]{1,0,2:T(8,128)S(1)} fusion(f32[16,32,128]{1,0,2:T(8,128)} %copy.31, f32[128,16,128]{2,1,0:T(8,128)S(1)} %get-tuple-element.5, s32[]{:T(128)S(6)} %select_n.29), kind=kLoop, calls=%fused_computation.6 | loop fusion | flops 720896 | bytes 786436 | tf_op jit(solution)/shard_map/add | solution.py:42
  141.7 1.1 copy.33
  142.8 1.7 %copy.29 = f32[4,32,768]{1,2,0:T(8,128)} copy(f32[4,32,768]{2,1,0:T(8,128)S(1)} %get-tuple-element.4) | data formatting | bytes 786432 | tf_op jit(solution)/shard_map/pallas_call | solution.py:627
  144.5 0.0 copy-start.10
  144.5 3.0 %copy.30 = f32[4,32,2,24,16]{3,4,0,2,1:T(8,128)S(1)} copy(f32[4,32,2,24,16]{1,4,3,2,0:T(8,128)} %bitcast.38) | data formatting | bytes 786432 | tf_op jit(solution)/shard_map/reshape | solution.py:672
  147.5 0.0 copy-done.10
  147.5 1.8 %convolution_bitcast_fusion = f32[16,32,128]{2,0,1:T(8,128)S(1)} fusion(f32[4,32,2,24,16]{3,4,0,2,1:T(8,128)S(1)} %copy.30, f32[4,2,24,128,1]{3,2,0,1,4:T(8,128)S(1)} %copy-done.10), kind=kOutput, calls=%fused_computation.1 | convolution fusion | flops 150994944 | bytes 753664 | tf_op jit(solution)/shard_map/syckx,sckz->xyz/dot_general | solution.py:673
  149.3 0.8 copy.32
  (7 shorter events, 0.1 us)
Async XLA Ops:
  0.6 6.1 %copy-start.1 = (bf16[128,768]{1,0:T(8,128)(2,1)S(1)}, bf16[128,768]{1,0:T(8,128)(2,1)}, u32[]{:S(2)}) copy-start(bf16[128,768]{1,0:T(8,128)(2,1)} %constant.57.clone.table_ref) | copy-start | bytes 589828
  6.8 3.4 %copy-start = (f32[2,2,32,128,128]{4,3,2,1,0:T(8,128)S(1)}, f32[2,2,32,128,128]{4,3,2,1,0:T(8,128)}, u32[]{:S(2)}) copy-start(f32[2,2,32,128,128]{4,3,2,1,0:T(8,128)} %high_ref.1) | copy-start | bytes 25165828
  10.2 5.8 %copy-start.11 = (f32[2]{0:T(128)S(1)}, f32[2]{0:T(128)}, u32[]{:S(2)}) copy-start(f32[2]{0:T(128)} %param.15) | copy-start | bytes 28
  10.2 5.9 %copy-start.2 = (bf16[1536,512]{1,0:T(8,128)(2,1)S(1)}, bf16[1536,512]{1,0:T(8,128)(2,1)}, u32[]{:S(2)}) copy-start(bf16[1536,512]{1,0:T(8,128)(2,1)} %constant.59.clone.right_ref) | copy-start | bytes 4718596
  10.2 5.9 %copy-start.3 = (bf16[256,768]{1,0:T(8,128)(2,1)S(1)}, bf16[256,768]{1,0:T(8,128)(2,1)}, u32[]{:S(2)}) copy-start(bf16[256,768]{1,0:T(8,128)(2,1)} %constant.62.clone.across_back_ref) | copy-start | bytes 1179652
  10.2 5.9 %copy-start.4 = (bf16[768,256]{1,0:T(8,128)(2,1)S(1)}, bf16[768,256]{1,0:T(8,128)(2,1)}, u32[]{:S(2)}) copy-start(bf16[768,256]{1,0:T(8,128)(2,1)} %constant.64.clone.along_back_ref) | copy-start | bytes 1179652
  10.2 5.9 %copy-start.5 = (f32[256,256]{1,0:T(8,128)S(1)}, f32[256,256]{1,0:T(8,128)}, u32[]{:S(2)}) copy-start(f32[256,256]{1,0:T(8,128)} %constant.61.clone.across_ref) | copy-start | bytes 786436
  10.2 5.9 %copy-start.6 = (f32[256,256]{1,0:T(8,128)S(1)}, f32[256,256]{1,0:T(8,128)}, u32[]{:S(2)}) copy-start(f32[256,256]{1,0:T(8,128)} %constant.63.clone.along_ref) | copy-start | bytes 786436
  10.2 5.9 %copy-start.7 = (bf16[256,240]{1,0:T(8,128)(2,1)S(1)}, bf16[256,240]{1,0:T(8,128)(2,1)}, u32[]{:S(2)}) copy-start(bf16[256,240]{1,0:T(8,128)(2,1)} %constant.58.clone.left_ref) | copy-start | bytes 368644
  10.2 5.9 %copy-start.8 = (f32[4,48,128]{2,1,0:T(8,128)S(1)}, f32[4,48,128]{2,1,0:T(8,128)}, u32[]{:S(2)}) copy-start(f32[4,48,128]{2,1,0:T(8,128)} %constant.60.clone.depth_ref) | copy-start | bytes 294916
  16.1 121.6 %copy-start.9 = (f32[16,32,128]{2,1,0:T(8,128)S(1)}, f32[16,32,128]{2,1,0:T(8,128)}, u32[]{:S(2)}) copy-start(f32[16,32,128]{2,1,0:T(8,128)} %param.16) | copy-start | bytes 786436
  144.5 3.0 %copy-start.10 = (f32[4,2,24,128,1]{3,2,0,1,4:T(8,128)S(1)}, f32[4,2,24,128,1]{3,2,0,1,4:T(8,128)}, u32[]{:S(2)}) copy-start(f32[4,2,24,128,1]{3,2,0,1,4:T(8,128)} %constant.68) | copy-start | bytes 294916

commit v4 on v3

--- a/solution.py
+++ b/solution.py
@@ -622,7 +622,7 @@
     *tables, backward = line_tables(extent, 4, peers)
     per_slab = tables[0].shape[1] // 2
     each = per_slab // peers
-    pieces = 4
+    pieces = 8
     vmem = pl.BlockSpec(memory_space=pltpu.VMEM)
     density, final = pl.pallas_call(
         density_kernel,

time: 152 us -> 151 us (level); the launches traced: 150 us -> 151 us
  no operation moved by 1% of the time
where the time goes in v4:
time: 151 us
  Pallas kernels  128 us (85%)
  local copies, waits for them, and re-layouts  13 us (9%)
  other arithmetic  4.8 us (3%)
  matrix products  3.47 us (2%)
    pallas_call x1, Pallas kernels, summed_density(): pl.pallas_call(density_kernel, in_specs=[pl.BlockSpec(memory_space=pl.ANY...  122 us
    unnamed x29, local copies, waits for them, and re-layouts  6.79 us
    pallas_call x1, Pallas kernels, transform_columns(): pl.pallas_call(column_kernel, grid=(rows // step,), in_specs=[pl.BlockSpe...  5.73 us

profile of v4, /device:TPU:0, one launch (start us, length us, event | category | flops | bytes accessed | tf_op | source)
XLA Modules:
  0.0 150.9 jit_solution(13135171811968797583)
XLA Ops:
  0.6 0.0 copy-start.1
  0.6 1.3 slice.31
  2.6 0.7 slice_multiply_fusion
  3.3 0.4 fusion.15
  3.7 0.4 convolution_add_fusion
  4.2 0.4 fusion.13
  4.6 0.4 convolution_subtract_fusion
  5.0 0.3 fusion.10
  5.3 0.3 fusion.11
  5.6 0.1 multiply_subtract_fusion
  5.8 0.7 dynamic-slice_convert_fusion
  6.5 0.1 fusion.34
  6.6 0.1 pad_maximum_fusion
  6.7 0.1 tile.10.mask_ref
  6.8 0.0 copy-done.1
  6.8 0.0 copy-start
  6.8 3.4 %copy-done = f32[2,2,32,128,128]{4,3,2,1,0:T(8,128)S(1)} copy-done((f32[2,2,32,128,128]{4,3,2,1,0:T(8,128)S(1)}, f32[2,2,32,128,128]{4,3,2,1,0:T(8,128)}, u32[]{:S(2)}) %copy-start) | copy-done | bytes 8388632
  10.2 0.0 copy-start.11
  10.2 0.0 copy-start.2
  10.2 0.0 copy-start.3
  10.2 0.0 copy-start.4
  10.2 0.0 copy-start.5
  10.2 0.0 copy-start.6
  10.2 0.0 copy-start.7
  10.2 0.0 copy-start.8
  10.2 5.7 %shard_map.140.columns_ref = f32[128,32,256]{2,1,0:T(8,128)S(1)} custom-call(f32[2,2,32,128,128]{4,3,2,1,0:T(8,128)S(1)} %copy-done, f32[2,2,32,128,128]{4,3,2,1,0:T(8,128)S(1)} %copy-done, f32[32,256]{1,0:T(8,128)S(1)} %tile.10.mask_ref, bf16[128,768]{1,0:T(8,128)(2,1)S(1)} %copy-done.1), custom_call_target="tpu_custom_call" | custom-call | flops 1610612736 | bytes 8388608 | tf_op jit(solution)/shard_map/pallas_call | solution.py:178
  16.0 0.0 copy-done.11
  16.0 0.1 broadcast_bitcast_fusion
  16.1 0.0 copy-done.2
  16.1 0.0 copy-done.3
  16.1 0.0 copy-done.4
  16.1 0.0 copy-done.5
  16.1 0.0 copy-done.6
  16.1 0.0 copy-done.7
  16.1 0.0 copy-done.8
  16.1 0.0 copy-start.9
  16.1 122.4 %shard_map.141 = (f32[128,16,128]{2,1,0:T(8,128)S(1)}, f32[4,32,768]{2,1,0:T(8,128)S(1)}) custom-call(f32[128,32,256]{2,1,0:T(8,128)S(1)} %shard_map.140.columns_ref, f32[128,512]{1,0:T(8,128)S(1)} %bitcast.36, f32[1,512]{1,0:T(1,128)S(1)} %bitcast.37, bf16[256,240]{1,0:T(8,128)(2,1)S(1)} %copy-done.7, bf16[1536,512]{1,0:T(8,128)(2,1)S(1)} %copy-done.2, ...), custom_call_target="tpu_custom_call" | custom-call | flops 6442450944 | bytes 4194304 | tf_op jit(solution)/shard_map/pallas_call | solution.py:627
  138.5 0.0 copy-done.9
  138.5 1.4 copy.31
  139.9 2.6 %fusion.2 = f32[16,32,128]{1,0,2:T(8,128)S(1)} fusion(f32[16,32,128]{1,0,2:T(8,128)} %copy.31, f32[128,16,128]{2,1,0:T(8,128)S(1)} %get-tuple-element.5, s32[]{:T(128)S(6)} %select_n.29), kind=kLoop, calls=%fused_computation.6 | loop fusion | flops 720896 | bytes 786436 | tf_op jit(solution)/shard_map/add | solution.py:42
  142.5 1.1 copy.33
  143.6 1.7 %copy.29 = f32[4,32,768]{1,2,0:T(8,128)} copy(f32[4,32,768]{2,1,0:T(8,128)S(1)} %get-tuple-element.4) | data formatting | bytes 786432 | tf_op jit(solution)/shard_map/pallas_call | solution.py:627
  145.3 0.0 copy-start.10
  145.3 3.0 %copy.30 = f32[4,32,2,24,16]{3,4,0,2,1:T(8,128)S(1)} copy(f32[4,32,2,24,16]{1,4,3,2,0:T(8,128)} %bitcast.38) | data formatting | bytes 786432 | tf_op jit(solution)/shard_map/reshape | solution.py:672
  148.2 0.0 copy-done.10
  148.3 1.8 %convolution_bitcast_fusion = f32[16,32,128]{2,0,1:T(8,128)S(1)} fusion(f32[4,32,2,24,16]{3,4,0,2,1:T(8,128)S(1)} %copy.30, f32[4,2,24,128,1]{3,2,0,1,4:T(8,128)S(1)} %copy-done.10), kind=kOutput, calls=%fused_computation.1 | convolution fusion | flops 150994944 | bytes 753664 | tf_op jit(solution)/shard_map/syckx,sckz->xyz/dot_general | solution.py:673
  150.1 0.8 copy.32
  (7 shorter events, 0.1 us)
Async XLA Ops:
  0.6 6.1 %copy-start.1 = (bf16[128,768]{1,0:T(8,128)(2,1)S(1)}, bf16[128,768]{1,0:T(8,128)(2,1)}, u32[]{:S(2)}) copy-start(bf16[128,768]{1,0:T(8,128)(2,1)} %constant.57.clone.table_ref) | copy-start | bytes 589828
  6.8 3.4 %copy-start = (f32[2,2,32,128,128]{4,3,2,1,0:T(8,128)S(1)}, f32[2,2,32,128,128]{4,3,2,1,0:T(8,128)}, u32[]{:S(2)}) copy-start(f32[2,2,32,128,128]{4,3,2,1,0:T(8,128)} %high_ref.1) | copy-start | bytes 25165828
  10.2 5.8 %copy-start.11 = (f32[2]{0:T(128)S(1)}, f32[2]{0:T(128)}, u32[]{:S(2)}) copy-start(f32[2]{0:T(128)} %param.15) | copy-start | bytes 28
  10.2 5.9 %copy-start.2 = (bf16[1536,512]{1,0:T(8,128)(2,1)S(1)}, bf16[1536,512]{1,0:T(8,128)(2,1)}, u32[]{:S(2)}) copy-start(bf16[1536,512]{1,0:T(8,128)(2,1)} %constant.59.clone.right_ref) | copy-start | bytes 4718596
  10.2 5.9 %copy-start.3 = (bf16[256,768]{1,0:T(8,128)(2,1)S(1)}, bf16[256,768]{1,0:T(8,128)(2,1)}, u32[]{:S(2)}) copy-start(bf16[256,768]{1,0:T(8,128)(2,1)} %constant.62.clone.across_back_ref) | copy-start | bytes 1179652
  10.2 5.9 %copy-start.4 = (bf16[768,256]{1,0:T(8,128)(2,1)S(1)}, bf16[768,256]{1,0:T(8,128)(2,1)}, u32[]{:S(2)}) copy-start(bf16[768,256]{1,0:T(8,128)(2,1)} %constant.64.clone.along_back_ref) | copy-start | bytes 1179652
  10.2 5.9 %copy-start.5 = (f32[256,256]{1,0:T(8,128)S(1)}, f32[256,256]{1,0:T(8,128)}, u32[]{:S(2)}) copy-start(f32[256,256]{1,0:T(8,128)} %constant.61.clone.across_ref) | copy-start | bytes 786436
  10.2 5.9 %copy-start.6 = (f32[256,256]{1,0:T(8,128)S(1)}, f32[256,256]{1,0:T(8,128)}, u32[]{:S(2)}) copy-start(f32[256,256]{1,0:T(8,128)} %constant.63.clone.along_ref) | copy-start | bytes 786436
  10.2 5.9 %copy-start.7 = (bf16[256,240]{1,0:T(8,128)(2,1)S(1)}, bf16[256,240]{1,0:T(8,128)(2,1)}, u32[]{:S(2)}) copy-start(bf16[256,240]{1,0:T(8,128)(2,1)} %constant.58.clone.left_ref) | copy-start | bytes 368644
  10.2 5.9 %copy-start.8 = (f32[4,48,128]{2,1,0:T(8,128)S(1)}, f32[4,48,128]{2,1,0:T(8,128)}, u32[]{:S(2)}) copy-start(f32[4,48,128]{2,1,0:T(8,128)} %constant.60.clone.depth_ref) | copy-start | bytes 294916
  16.1 122.4 %copy-start.9 = (f32[16,32,128]{2,1,0:T(8,128)S(1)}, f32[16,32,128]{2,1,0:T(8,128)}, u32[]{:S(2)}) copy-start(f32[16,32,128]{2,1,0:T(8,128)} %param.16) | copy-start | bytes 786436
  145.3 3.0 %copy-start.10 = (f32[4,2,24,128,1]{3,2,0,1,4:T(8,128)S(1)}, f32[4,2,24,128,1]{3,2,0,1,4:T(8,128)}, u32[]{:S(2)}) copy-start(f32[4,2,24,128,1]{3,2,0,1,4:T(8,128)} %constant.68) | copy-start | bytes 294916
